TPU v7x, 32 devices: a whole 2x2x4 slice. The times are simulated.
32 devices in a mesh: groups: 2 (over x), gy: 16 (over z, y, core).
Axes of the slice: x: 2, y: 2, z: 4, core: 2. Of those that a mesh axis runs over, the one named last changes fastest.
Arguments:
- observed: float32 [2048, 16, 256], P(('groups', 'gy')), parts along dimension 0, may hold values from -6 to 6
- tf_table: float32 [16], replicated, may hold values from 0.2 to 2
- tilt_index: int32 [513, 129], replicated, may hold values from 0 to 15
- wedge: int32 [513, 129], replicated, may hold values 0 or 1
Outputs:
- restored: float32 [2048, 16, 256], P(('groups', 'gy')), parts along dimension 0
There are 2 independent parts, one for each index of `groups`. A program takes and returns all parts, laid end to end along the dimension named above; an argument that names none is the same for every part. Nothing has to cross between parts.
All inputs are finite; a program needn't handle non-finite values.
Results may differ from a plain program's by a relative error of at most 0.00011.
Values sent between devices are 32-bit elements; how exact they have to be, the bound alone decides.
No kernel may reach another device: no remote copies, remote signals or barrier semaphores. Data moves between devices by JAX's collectives and lax.ppermute only.
A program may use at most 64 MiB of HBM per device.

v0:
```python
import math

import jax
import jax.numpy as jnp
from jax import lax
from jax.sharding import PartitionSpec as P

NX = 1024
OUTER = 2
PASSES = 2


step_dual = 0.14
step_primal = 0.14
huber_eps = 0.05
bound_dual = 0.5
highest = lax.Precision.HIGHEST


def extended(value, sides, width):
    for axis, dim in sides:
        devices, length = (lax.axis_size(axis), value.shape[dim])
        up = [(i, (i + 1) % devices) for i in range(devices - 1)]
        down = [(j, i) for i, j in up]
        last = lax.slice_in_dim(value, length - width, length, axis=dim)
        initial = lax.slice_in_dim(value, 0, width, axis=dim)
        before = lax.ppermute(last, axis, up)
        after = lax.ppermute(initial, axis, down)
        value = jnp.concatenate([before, value, after], axis=dim)
    return value


def curvature(field, axis):
    widths = [(0, 0), (0, 0), (0, 0)]
    widths[axis] = (1, 1)
    padded = jnp.pad(field, widths)
    upper = lax.slice_in_dim(padded, 2, padded.shape[axis], axis=axis)
    lower = lax.slice_in_dim(padded, 0, padded.shape[axis] - 2, axis=axis)
    return upper + lower - 2.0 * field


def rim_curvature(padded, field, axis):
    upper = lax.slice_in_dim(padded, 2, padded.shape[axis], axis=axis)
    lower = lax.slice_in_dim(padded, 0, padded.shape[axis] - 2, axis=axis)
    return upper + lower - 2.0 * field


def denoise(target, duals, sharded, primal_rim, dual_rim):
    field = target
    lead = target
    for sweep in range(PASSES):
        padded = primal_rim(lead)
        raised = []
        for axis in range(3):
            if axis == sharded:
                bend = rim_curvature(padded, lead, axis)
            else:
                bend = curvature(lead, axis)
            raised.append(
                (duals[axis] + step_dual * bend) / (1.0 + step_dual * huber_eps / bound_dual)
            )
        total = raised[0] * raised[0] + raised[1] * raised[1] + raised[2] * raised[2]
        shrink = jnp.sqrt(jnp.maximum(1.0, total / (bound_dual * bound_dual)))
        duals = (raised[0] / shrink, raised[1] / shrink, raised[2] / shrink)
        padded_dual = dual_rim(duals[sharded])
        adjoint = jnp.zeros_like(field)
        for axis in range(3):
            if axis == sharded:
                adjoint = rim_curvature(padded_dual, duals[axis], axis)
            else:
                adjoint = adjoint + curvature(duals[axis], axis)
        updated = (field - step_primal * adjoint + step_primal * target) / (1.0 + step_primal)
        lead = 2.0 * updated - field
        field = updated
    return (field, duals)


def z_tables(length):
    half = length // 2
    position = jnp.arange(length, dtype=jnp.int32)
    column = jnp.arange(length, dtype=jnp.int32)
    is_cosine = column <= half
    frequency = jnp.where(is_cosine, column, column - half)
    phase = position[:, None] * frequency[None, :] % length
    angle = phase.astype(jnp.float32) * (2.0 * math.pi / length)
    forward = jnp.where(is_cosine[None, :], jnp.cos(angle), jnp.sin(angle))
    weight = jnp.where((column == 0) | (column == half), 1.0, 2.0) / length
    backward = forward.T * weight[:, None]
    return (forward, backward)


def x_tables(length):
    half = length // 2
    freqs = jnp.arange(half + 1, dtype=jnp.int32)
    position = jnp.arange(length, dtype=jnp.int32)
    phase = freqs[:, None] * position[None, :] % length
    angle = phase.astype(jnp.float32) * (2.0 * math.pi / length)
    cos_table = jnp.cos(angle)
    sin_table = jnp.sin(angle)
    weight = jnp.where((freqs == 0) | (freqs == half), 1.0, 2.0) / length
    return (cos_table, sin_table, (cos_table * weight[:, None]).T, (sin_table * weight[:, None]).T)


def x_forward(columns, cos_table, sin_table):
    flat = columns.reshape(columns.shape[0], -1)
    shape_out = (cos_table.shape[0],) + columns.shape[1:]
    real_part = jnp.dot(cos_table, flat, precision=highest).reshape(shape_out)
    imag_part = jnp.dot(sin_table, flat, precision=highest).reshape(shape_out)
    return (real_part, imag_part)


def x_inverse(real_part, imag_part, cos_back, sin_back):
    rows = real_part.shape[0]
    flat_real = real_part.reshape(rows, -1)
    flat_imag = imag_part.reshape(rows, -1)
    summed = jnp.dot(cos_back, flat_real, precision=highest) + jnp.dot(
        sin_back, flat_imag, precision=highest
    )
    return summed.reshape((cos_back.shape[0],) + real_part.shape[1:])


def filters(tf_table, tilt_index, wedge, length_z):
    levels = jnp.arange(tf_table.shape[0], dtype=jnp.int32)
    picked = jnp.sum(jnp.where(tilt_index[:, :, None] == levels, tf_table, 0.0), axis=2)
    half_rows = picked * wedge.astype(jnp.float32)
    response = jnp.concatenate([half_rows, half_rows[:, 1 : length_z // 2]], 1)
    denom = response * response + 1.0
    return ((response / denom)[:, None, :], (1.0 / denom)[:, None, :])


def rim_x_primal(field):
    return extended(field, (("gy", 0),), 1)


def rim_x_dual(field):
    return extended(field, (("gy", 0),), 1)


def local(observed, tf_table, tilt_index, wedge):
    length_z = observed.shape[2]
    forward_z, backward_z = z_tables(length_z)
    cos_table, sin_table, cos_back, sin_back = x_tables(NX)
    g_data, g_prior = filters(tf_table, tilt_index, wedge, length_z)
    packed = jnp.dot(observed, forward_z, precision=highest)
    columns = lax.all_to_all(packed, "gy", split_axis=1, concat_axis=0, tiled=True)
    data_real, data_imag = x_forward(columns, cos_table, sin_table)
    prior_real, prior_imag = (data_real, data_imag)
    current = observed
    duals = (jnp.zeros_like(observed), jnp.zeros_like(observed), jnp.zeros_like(observed))
    for outer in range(OUTER):
        if outer > 0:
            again = lax.all_to_all(
                jnp.dot(current, forward_z, precision=highest),
                "gy",
                split_axis=1,
                concat_axis=0,
                tiled=True,
            )
            prior_real, prior_imag = x_forward(again, cos_table, sin_table)
        merged = x_inverse(
            g_data * data_real + g_prior * prior_real,
            g_data * data_imag + g_prior * prior_imag,
            cos_back,
            sin_back,
        )
        slabs = lax.all_to_all(merged, "gy", split_axis=0, concat_axis=1, tiled=True)
        target = jnp.dot(slabs, backward_z, precision=highest)
        current, duals = denoise(target, duals, 0, rim_x_primal, rim_x_dual)
    return current


def solution(mesh):
    in_specs = (P(("groups", "gy"), None, None), P(), P(), P())
    out_specs = P(("groups", "gy"), None, None)
    return jax.shard_map(local, mesh=mesh, in_specs=in_specs, out_specs=out_specs, check_vma=False)
```

profile of v0, /device:TPU:8, one launch (start us, length us, event | category | flops | bytes accessed | tf_op | source)
XLA Modules:
  0.0 304.3 jit_solution(17991332169227890438)
XLA Ops:
  1.2 3.4 %convolution_bitcast_fusion = f32[64,16,256]{2,0,1:T(8,128)} fusion(f32[64,16,256]{2,1,0:T(8,128)S(1)} %copy-done, s32[256]{0:T(256)S(1)} %add_select_fusion.3, pred[256]{0:T(512)(128)(4,1)S(1)} %iota_compare_fusion.3), kind=kOutput, calls=%fused_computation.55 | convolution fusion | flops 806289408 | bytes 2098432 | tf_op jit(solution)/shard_map/dot_general | solution.py:144
  4.7 6.9 %all-to-all-start = ((f32[64,16,256]{2,0,1:T(8,128)}), f32[64,16,256]{2,0,1:T(8,128)S(1)}, u32[]{:S(2)}, u32[]{:S(2)}) async-start(f32[64,16,256]{2,0,1:T(8,128)} %convolution_bitcast_fusion), calls=%async_computation | async-start | bytes 2097152 | tf_op jit(solution)/shard_map/all_to_all | solution.py:145
  13.5 21.9 %all-to-all-done = f32[64,16,256]{2,0,1:T(8,128)S(1)} async-done(((f32[64,16,256]{2,0,1:T(8,128)}), f32[64,16,256]{2,0,1:T(8,128)S(1)}, u32[]{:S(2)}, u32[]{:S(2)}) %all-to-all-start) | async-done | bytes 1048608 | tf_op jit(solution)/shard_map/all_to_all | solution.py:145
  35.3 10.8 %fusion.41 = f32[513,256]{0,1:T(8,128)S(1)} fusion(f32[1024,256]{1,0:T(8,128)S(1)} %bitcast.46), kind=kOutput, calls=%fused_computation.67 | convolution fusion | flops 1621112832 | bytes 1573888 | tf_op jit(solution)/shard_map/dot_general | solution.py:108
  46.1 10.5 %fusion.36 = f32[513,256]{0,1:T(8,128)S(1)} fusion(f32[1024,256]{1,0:T(8,128)S(1)} %bitcast.47), kind=kOutput, calls=%fused_computation.66 | convolution fusion | flops 1621112832 | bytes 1573888 | tf_op jit(solution)/shard_map/dot_general | solution.py:107
  56.6 12.6 %fusion.8 = f32[1024,256]{1,0:T(8,128)S(1)} fusion(f32[513]{0:T(1024)S(1)} %select_multiply_fusion.3, f32[513,256]{0,1:T(8,128)S(1)} %fusion.41, f32[513,127]{0,1:T(8,128)S(1)} %slice.276, f32[513,129]{0,1:T(8,128)S(1)} %convert_multiply_fusion), kind=kOutput, calls=%fused_computation.13 | convolution fusion | flops 1622688768 | bytes 2101252 | tf_op jit(solution)/shard_map/dot_general | solution.py:116
  69.3 12.1 %fusion.17 = f32[1024,1,256]{2,0,1:T(8,128)S(1)} fusion(f32[1024,256]{1,0:T(8,128)S(1)} %fusion.8, f32[513]{0:T(1024)S(1)} %select_multiply_fusion.3, f32[513,256]{0,1:T(8,128)S(1)} %fusion.36, f32[513,127]{0,1:T(8,128)S(1)} %slice.276, f32[513,129]{0,1:T(8,128)S(1)} %convert_multiply_fusion), kind=kOutput, calls=%fused_computation.52 | convolution fusion | flops 1622950912 | bytes 3149828 | tf_op jit(solution)/shard_map/dot_general | solution.py:116
  83.5 5.6 %all-to-all-start.1 = ((f32[1024,1,256]{2,1,0:T(1,128)}), f32[1024,1,256]{2,1,0:T(1,128)S(1)}, u32[]{:S(2)}, u32[]{:S(2)}) async-start(f32[1024,1,256]{2,1,0:T(1,128)} %copy.43), calls=%async_computation.1 | async-start | bytes 2097152 | tf_op jit(solution)/shard_map/all_to_all | solution.py:166
  89.0 24.2 %all-to-all-done.1 = f32[1024,1,256]{2,1,0:T(1,128)S(1)} async-done(((f32[1024,1,256]{2,1,0:T(1,128)}), f32[1024,1,256]{2,1,0:T(1,128)S(1)}, u32[]{:S(2)}, u32[]{:S(2)}) %all-to-all-start.1) | async-done | bytes 1048608 | tf_op jit(solution)/shard_map/all_to_all | solution.py:166
  113.3 2.6 fusion.146
  120.6 3.7 %collective-permute-done.1 = f32[1,16,256]{2,1,0:T(8,128)S(1)} collective-permute-done((f32[1,16,256]{2,1,0:T(8,128)S(1)}, f32[1,16,256]{2,1,0:T(8,128)S(1)}, u32[]{:S(2)}, u32[]{:S(2)}) %collective-permute-start.1) | collective-permute-done | bytes 16416 | tf_op jit(solution)/shard_map/ppermute | solution.py:27
  127.5 2.4 collective-permute-start.3
  130.7 2.7 collective-permute-done.3
  136.4 2.4 collective-permute-start.5
  138.8 3.5 %collective-permute-done.5 = f32[1,16,256]{2,1,0:T(8,128)S(1)} collective-permute-done((f32[1,16,256]{2,1,0:T(8,128)S(1)}, f32[1,16,256]{2,1,0:T(8,128)S(1)}, u32[]{:S(2)}, u32[]{:S(2)}) %collective-permute-start.5) | collective-permute-done | bytes 16416 | tf_op jit(solution)/shard_map/ppermute | solution.py:27
  145.8 2.4 collective-permute-start.7
  148.7 3.1 %collective-permute-done.7 = f32[1,16,256]{2,1,0:T(8,128)S(1)} collective-permute-done((f32[1,16,256]{2,1,0:T(8,128)S(1)}, f32[1,16,256]{2,1,0:T(8,128)S(1)}, u32[]{:S(2)}, u32[]{:S(2)}) %collective-permute-start.7) | collective-permute-done | bytes 16416 | tf_op jit(solution)/shard_map/ppermute | solution.py:27
  152.8 2.5 fusion.148
  155.4 30.5 %all_to_all.66 = f32[64,16,256]{2,0,1:T(8,128)S(1)} all-to-all(f32[64,16,256]{2,0,1:T(8,128)S(1)} %fusion.148), channel_id=1, replica_groups=mesh['groups'=2,'gy'=16] {'gy'}, dimensions={1} | all-to-all | bytes 2097152 | tf_op jit(solution)/shard_map/all_to_all | solution.py:152
  185.9 10.7 %fusion.26 = f32[513,256]{0,1:T(8,128)S(1)} fusion(f32[1024,256]{1,0:T(8,128)S(1)} %bitcast.48, f32[513,256]{0,1:T(8,128)S(1)} %copy-done.5, f32[513,127]{0,1:T(8,128)S(1)} %slice.276, f32[513,129]{0,1:T(8,128)S(1)} %convert_multiply_fusion), kind=kOutput, calls=%fused_computation.57 | convolution fusion | flops 1622163456 | bytes 2624512 | tf_op jit(solution)/shard_map/dot_general | solution.py:108
  196.5 10.7 %fusion.27 = f32[513,256]{0,1:T(8,128)S(1)} fusion(f32[1024,256]{1,0:T(8,128)S(1)} %bitcast.49, f32[513,256]{0,1:T(8,128)S(1)} %fusion.36, f32[513,127]{0,1:T(8,128)S(1)} %slice.276, f32[513,129]{0,1:T(8,128)S(1)} %convert_multiply_fusion), kind=kOutput, calls=%fused_computation.59 | convolution fusion | flops 1622163456 | bytes 2624512 | tf_op jit(solution)/shard_map/dot_general | solution.py:107
  207.3 12.1 %fusion.6 = f32[1024,256]{1,0:T(8,128)S(1)} fusion(f32[513,256]{0,1:T(8,128)S(1)} %fusion.26, f32[513]{0:T(1024)S(1)} %select_multiply_fusion.3), kind=kOutput, calls=%fused_computation.11 | convolution fusion | flops 1621638144 | bytes 1575940 | tf_op jit(solution)/shard_map/dot_general | solution.py:116
  219.4 12.3 %fusion.23 = f32[1024,1,256]{2,0,1:T(8,128)S(1)} fusion(f32[1024,256]{1,0:T(8,128)S(1)} %fusion.6, f32[513,256]{0,1:T(8,128)S(1)} %fusion.27, f32[513]{0:T(1024)S(1)} %select_multiply_fusion.3), kind=kOutput, calls=%fused_computation.54 | convolution fusion | flops 1621900288 | bytes 2624516 | tf_op jit(solution)/shard_map/dot_general | solution.py:116
  233.0 29.6 %all_to_all.67 = f32[1024,1,256]{2,1,0:T(1,128)S(1)} all-to-all(f32[1024,1,256]{2,1,0:T(1,128)S(1)} %copy.48), channel_id=1, replica_groups=mesh['groups'=2,'gy'=16] {'gy'}, dimensions={0} | all-to-all | bytes 2097152 | tf_op jit(solution)/shard_map/all_to_all | solution.py:166
  262.7 2.6 fusion.144
  265.3 3.0 %collective-permute-start.8 = (f32[1,16,256]{2,1,0:T(8,128)S(1)}, f32[1,16,256]{2,1,0:T(8,128)S(1)}, u32[]{:S(2)}, u32[]{:S(2)}) collective-permute-start(f32[1,16,256]{2,1,0:T(8,128)S(1)} %get-tuple-element.35), channel_id=1, source_target_pairs={{1,0},{2,1},{3,2},{4,3},{5,4},{6,5},{7,6},{8,7},{9,8},{10,9},{11,1... | collective-permute-start | bytes 49160 | tf_op jit(solution)/shard_map/ppermute | solution.py:28
  270.3 4.0 %collective-permute-done.9 = f32[1,16,256]{2,1,0:T(8,128)S(1)} collective-permute-done((f32[1,16,256]{2,1,0:T(8,128)S(1)}, f32[1,16,256]{2,1,0:T(8,128)S(1)}, u32[]{:S(2)}, u32[]{:S(2)}) %collective-permute-start.9) | collective-permute-done | bytes 16416 | tf_op jit(solution)/shard_map/ppermute | solution.py:27
  277.8 2.4 collective-permute-start.11
  280.7 3.1 %collective-permute-done.11 = f32[1,16,256]{2,1,0:T(8,128)S(1)} collective-permute-done((f32[1,16,256]{2,1,0:T(8,128)S(1)}, f32[1,16,256]{2,1,0:T(8,128)S(1)}, u32[]{:S(2)}, u32[]{:S(2)}) %collective-permute-start.11) | collective-permute-done | bytes 16416 | tf_op jit(solution)/shard_map/ppermute | solution.py:27
  286.7 2.4 collective-permute-start.13
  289.1 3.5 %collective-permute-done.13 = f32[1,16,256]{2,1,0:T(8,128)S(1)} collective-permute-done((f32[1,16,256]{2,1,0:T(8,128)S(1)}, f32[1,16,256]{2,1,0:T(8,128)S(1)}, u32[]{:S(2)}, u32[]{:S(2)}) %collective-permute-start.13) | collective-permute-done | bytes 16416 | tf_op jit(solution)/shard_map/ppermute | solution.py:27
  299.0 3.1 %collective-permute-done.15 = f32[1,16,256]{2,1,0:T(8,128)S(1)} collective-permute-done((f32[1,16,256]{2,1,0:T(8,128)S(1)}, f32[1,16,256]{2,1,0:T(8,128)S(1)}, u32[]{:S(2)}, u32[]{:S(2)}) %collective-permute-start.15) | collective-permute-done | bytes 16416 | tf_op jit(solution)/shard_map/ppermute | solution.py:27
  (61 shorter events, 40.0 us)
Async XLA Ops:
  0.0 1.2 copy-start
  4.7 6.9 %copy-start.1 = (s32[513,129]{0,1:T(8,128)S(1)}, s32[513,129]{0,1:T(8,128)}, u32[]{:S(2)}) copy-start(s32[513,129]{0,1:T(8,128)} %param.6) | copy-start | bytes 794128
  4.7 6.9 %copy-start.3 = (f32[16]{0:T(128)S(1)}, f32[16]{0:T(128)}, u32[]{:S(2)}) copy-start(f32[16]{0:T(128)} %param.5) | copy-start | bytes 196
  4.7 8.7 %copy-start.2 = (s32[513,129]{0,1:T(8,128)S(1)}, s32[513,129]{0,1:T(8,128)}, u32[]{:S(2)}) copy-start(s32[513,129]{0,1:T(8,128)} %param.7) | copy-start | bytes 794128
  4.7 30.7 %all-to-all-start = ((f32[64,16,256]{2,0,1:T(8,128)}), f32[64,16,256]{2,0,1:T(8,128)S(1)}, u32[]{:S(2)}, u32[]{:S(2)}) async-start(f32[64,16,256]{2,0,1:T(8,128)} %convolution_bitcast_fusion), calls=%async_computation | async-start | bytes 2097152 | tf_op jit(solution)/shard_map/all_to_all | solution.py:145
  46.1 10.5 %copy-start.4 = (f32[513,256]{0,1:T(8,128)}, f32[513,256]{0,1:T(8,128)S(1)}, u32[]{:S(2)}) copy-start(f32[513,256]{0,1:T(8,128)S(1)} %fusion.41) | copy-start | bytes 1575940
  83.5 29.8 %all-to-all-start.1 = ((f32[1024,1,256]{2,1,0:T(1,128)}), f32[1024,1,256]{2,1,0:T(1,128)S(1)}, u32[]{:S(2)}, u32[]{:S(2)}) async-start(f32[1024,1,256]{2,1,0:T(1,128)} %copy.43), calls=%async_computation.1 | async-start | bytes 2097152 | tf_op jit(solution)/shard_map/all_to_all | solution.py:166
  116.0 4.6 %collective-permute-start = (f32[1,16,256]{2,1,0:T(8,128)S(1)}, f32[1,16,256]{2,1,0:T(8,128)S(1)}, u32[]{:S(2)}, u32[]{:S(2)}) collective-permute-start(f32[1,16,256]{2,1,0:T(8,128)S(1)} %get-tuple-element.45), channel_id=1, source_target_pairs={{1,0},{2,1},{3,2},{4,3},{5,4},{6,5},{7,6},{8,7},{9,8},{10,9},{11,1... | collective-permute-start | bytes 49160 | tf_op jit(solution)/shard_map/ppermute | solution.py:28
  118.3 6.0 %collective-permute-start.1 = (f32[1,16,256]{2,1,0:T(8,128)S(1)}, f32[1,16,256]{2,1,0:T(8,128)S(1)}, u32[]{:S(2)}, u32[]{:S(2)}) collective-permute-start(f32[1,16,256]{2,1,0:T(8,128)S(1)} %get-tuple-element.46), channel_id=1, source_target_pairs={{0,1},{1,2},{2,3},{3,4},{4,5},{5,6},{6,7},{7,8},{8,9},{9,10},{10,1... | collective-permute-start | bytes 49160 | tf_op jit(solution)/shard_map/ppermute | solution.py:27
  125.6 5.1 %collective-permute-start.2 = (f32[1,16,256]{2,1,0:T(8,128)S(1)}, f32[1,16,256]{2,1,0:T(8,128)S(1)}, u32[]{:S(2)}, u32[]{:S(2)}) collective-permute-start(f32[1,16,256]{2,1,0:T(8,128)S(1)} %get-tuple-element.43), channel_id=1, source_target_pairs={{1,0},{2,1},{3,2},{4,3},{5,4},{6,5},{7,6},{8,7},{9,8},{10,9},{11,1... | collective-permute-start | bytes 49160 | tf_op jit(solution)/shard_map/ppermute | solution.py:28
  127.5 6.0 %collective-permute-start.3 = (f32[1,16,256]{2,1,0:T(8,128)S(1)}, f32[1,16,256]{2,1,0:T(8,128)S(1)}, u32[]{:S(2)}, u32[]{:S(2)}) collective-permute-start(f32[1,16,256]{2,1,0:T(8,128)S(1)} %get-tuple-element.44), channel_id=1, source_target_pairs={{0,1},{1,2},{2,3},{3,4},{4,5},{5,6},{6,7},{7,8},{8,9},{9,10},{10,1... | collective-permute-start | bytes 49160 | tf_op jit(solution)/shard_map/ppermute | solution.py:27
  134.4 4.3 %collective-permute-start.4 = (f32[1,16,256]{2,1,0:T(8,128)S(1)}, f32[1,16,256]{2,1,0:T(8,128)S(1)}, u32[]{:S(2)}, u32[]{:S(2)}) collective-permute-start(f32[1,16,256]{2,1,0:T(8,128)S(1)} %get-tuple-element.41), channel_id=1, source_target_pairs={{1,0},{2,1},{3,2},{4,3},{5,4},{6,5},{7,6},{8,7},{9,8},{10,9},{11,1... | collective-permute-start | bytes 49160 | tf_op jit(solution)/shard_map/ppermute | solution.py:28
  136.4 6.0 %collective-permute-start.5 = (f32[1,16,256]{2,1,0:T(8,128)S(1)}, f32[1,16,256]{2,1,0:T(8,128)S(1)}, u32[]{:S(2)}, u32[]{:S(2)}) collective-permute-start(f32[1,16,256]{2,1,0:T(8,128)S(1)} %get-tuple-element.42), channel_id=1, source_target_pairs={{0,1},{1,2},{2,3},{3,4},{4,5},{5,6},{6,7},{7,8},{8,9},{9,10},{10,1... | collective-permute-start | bytes 49160 | tf_op jit(solution)/shard_map/ppermute | solution.py:27
  143.9 4.8 %collective-permute-start.6 = (f32[1,16,256]{2,1,0:T(8,128)S(1)}, f32[1,16,256]{2,1,0:T(8,128)S(1)}, u32[]{:S(2)}, u32[]{:S(2)}) collective-permute-start(f32[1,16,256]{2,1,0:T(8,128)S(1)} %get-tuple-element.37), channel_id=1, source_target_pairs={{1,0},{2,1},{3,2},{4,3},{5,4},{6,5},{7,6},{8,7},{9,8},{10,9},{11,1... | collective-permute-start | bytes 49160 | tf_op jit(solution)/shard_map/ppermute | solution.py:28
  145.8 6.0 %collective-permute-start.7 = (f32[1,16,256]{2,1,0:T(8,128)S(1)}, f32[1,16,256]{2,1,0:T(8,128)S(1)}, u32[]{:S(2)}, u32[]{:S(2)}) collective-permute-start(f32[1,16,256]{2,1,0:T(8,128)S(1)} %get-tuple-element.38), channel_id=1, source_target_pairs={{0,1},{1,2},{2,3},{3,4},{4,5},{5,6},{6,7},{7,8},{8,9},{9,10},{10,1... | collective-permute-start | bytes 49160 | tf_op jit(solution)/shard_map/ppermute | solution.py:27
  155.4 30.5 %copy-start.5 = (f32[513,256]{0,1:T(8,128)S(1)}, f32[513,256]{0,1:T(8,128)}, u32[]{:S(2)}) copy-start(f32[513,256]{0,1:T(8,128)} %copy-done.4) | copy-start | bytes 1575940
  265.3 5.0 %collective-permute-start.8 = (f32[1,16,256]{2,1,0:T(8,128)S(1)}, f32[1,16,256]{2,1,0:T(8,128)S(1)}, u32[]{:S(2)}, u32[]{:S(2)}) collective-permute-start(f32[1,16,256]{2,1,0:T(8,128)S(1)} %get-tuple-element.35), channel_id=1, source_target_pairs={{1,0},{2,1},{3,2},{4,3},{5,4},{6,5},{7,6},{8,7},{9,8},{10,9},{11,1... | collective-permute-start | bytes 49160 | tf_op jit(solution)/shard_map/ppermute | solution.py:28
  268.4 6.0 %collective-permute-start.9 = (f32[1,16,256]{2,1,0:T(8,128)S(1)}, f32[1,16,256]{2,1,0:T(8,128)S(1)}, u32[]{:S(2)}, u32[]{:S(2)}) collective-permute-start(f32[1,16,256]{2,1,0:T(8,128)S(1)} %get-tuple-element.36), channel_id=1, source_target_pairs={{0,1},{1,2},{2,3},{3,4},{4,5},{5,6},{6,7},{7,8},{8,9},{9,10},{10,1... | collective-permute-start | bytes 49160 | tf_op jit(solution)/shard_map/ppermute | solution.py:27
  275.9 4.8 %collective-permute-start.10 = (f32[1,16,256]{2,1,0:T(8,128)S(1)}, f32[1,16,256]{2,1,0:T(8,128)S(1)}, u32[]{:S(2)}, u32[]{:S(2)}) collective-permute-start(f32[1,16,256]{2,1,0:T(8,128)S(1)} %get-tuple-element.31), channel_id=1, source_target_pairs={{1,0},{2,1},{3,2},{4,3},{5,4},{6,5},{7,6},{8,7},{9,8},{10,9},{11,1... | collective-permute-start | bytes 49160 | tf_op jit(solution)/shard_map/ppermute | solution.py:28
  277.8 6.0 %collective-permute-start.11 = (f32[1,16,256]{2,1,0:T(8,128)S(1)}, f32[1,16,256]{2,1,0:T(8,128)S(1)}, u32[]{:S(2)}, u32[]{:S(2)}) collective-permute-start(f32[1,16,256]{2,1,0:T(8,128)S(1)} %get-tuple-element.32), channel_id=1, source_target_pairs={{0,1},{1,2},{2,3},{3,4},{4,5},{5,6},{6,7},{7,8},{8,9},{9,10},{10,1... | collective-permute-start | bytes 49160 | tf_op jit(solution)/shard_map/ppermute | solution.py:27
  284.8 4.3 %collective-permute-start.12 = (f32[1,16,256]{2,1,0:T(8,128)S(1)}, f32[1,16,256]{2,1,0:T(8,128)S(1)}, u32[]{:S(2)}, u32[]{:S(2)}) collective-permute-start(f32[1,16,256]{2,1,0:T(8,128)S(1)} %get-tuple-element.29), channel_id=1, source_target_pairs={{1,0},{2,1},{3,2},{4,3},{5,4},{6,5},{7,6},{8,7},{9,8},{10,9},{11,1... | collective-permute-start | bytes 49160 | tf_op jit(solution)/shard_map/ppermute | solution.py:28
  286.7 6.0 %collective-permute-start.13 = (f32[1,16,256]{2,1,0:T(8,128)S(1)}, f32[1,16,256]{2,1,0:T(8,128)S(1)}, u32[]{:S(2)}, u32[]{:S(2)}) collective-permute-start(f32[1,16,256]{2,1,0:T(8,128)S(1)} %get-tuple-element.30), channel_id=1, source_target_pairs={{0,1},{1,2},{2,3},{3,4},{4,5},{5,6},{6,7},{7,8},{8,9},{9,10},{10,1... | collective-permute-start | bytes 49160 | tf_op jit(solution)/shard_map/ppermute | solution.py:27
  294.2 4.8 %collective-permute-start.14 = (f32[1,16,256]{2,1,0:T(8,128)S(1)}, f32[1,16,256]{2,1,0:T(8,128)S(1)}, u32[]{:S(2)}, u32[]{:S(2)}) collective-permute-start(f32[1,16,256]{2,1,0:T(8,128)S(1)} %get-tuple-element.25), channel_id=1, source_target_pairs={{1,0},{2,1},{3,2},{4,3},{5,4},{6,5},{7,6},{8,7},{9,8},{10,9},{11,1... | collective-permute-start | bytes 49160 | tf_op jit(solution)/shard_map/ppermute | solution.py:28
  296.1 6.0 %collective-permute-start.15 = (f32[1,16,256]{2,1,0:T(8,128)S(1)}, f32[1,16,256]{2,1,0:T(8,128)S(1)}, u32[]{:S(2)}, u32[]{:S(2)}) collective-permute-start(f32[1,16,256]{2,1,0:T(8,128)S(1)} %get-tuple-element.26), channel_id=1, source_target_pairs={{0,1},{1,2},{2,3},{3,4},{4,5},{5,6},{6,7},{7,8},{8,9},{9,10},{10,1... | collective-permute-start | bytes 49160 | tf_op jit(solution)/shard_map/ppermute | solution.py:27
where the time goes:
time: 308 us; the launch traced here: 304 us
  matrix products  103 us (33%)
  waiting for transfers between devices  72.9 us (24%)
  blocking collectives  60.1 us (20%)
  starting transfers between devices  48 us (16%)
  other arithmetic  14.8 us (5%)
  local copies, waits for them, and re-layouts  4.73 us (2%)
    all_to_all x1, blocking collectives, local(): lax.all_to_all(jnp.dot(current, forward_z, precision=highest), 'gy', spli...  30.5 us
    all_to_all x1, blocking collectives, local(): lax.all_to_all(merged, 'gy', split_axis=0, concat_axis=1, tiled=True)  29.6 us
    ppermute x8, waiting for transfers between devices, extended(): before = lax.ppermute(last, axis, up)  26.8 us
    dot_general x2, matrix products, x_inverse(): jnp.dot(sin_back, flat_imag, precision=highest)  24.8 us
    dot_general x2, matrix products, x_inverse(): jnp.dot(cos_back, flat_real, precision=highest)  24.4 us
    all_to_all x1, waiting for transfers between devices, local(): lax.all_to_all(merged, 'gy', split_axis=0, concat_axis=1, tiled=True)  24.2 us
    all_to_all x1, waiting for transfers between devices, local(): lax.all_to_all(packed, 'gy', split_axis=1, concat_axis=0, tiled=True)  21.9 us
    dot_general x2, matrix products, x_forward(): imag_part = jnp.dot(sin_table, flat, precision=highest).reshape(shape_out)  21.4 us
  transfers between devices with their start and end apart: 18, of which 10 were waited for; matrix products, arithmetic and copies ran while one was open for 1% of the time, Pallas kernels for 0%

commit v1 on v0

v1 whole, which is shorter than its diff:
```python
import functools

import jax
import jax.numpy as jnp
import ml_dtypes
import numpy as np
from jax import lax
from jax.experimental import pallas as pl
from jax.experimental.pallas import tpu as pltpu
from jax.sharding import PartitionSpec as P

OUTER = 2
PASSES = 2

step_dual = 0.14
step_primal = 0.14
huber_eps = 0.05
bound_dual = 0.5

SUB = 8
LANE = 128
HALO_LAST = 4
HALO_FIRST = 8
VMEM_LIMIT = 48 * 1024 * 1024

f32 = jnp.float32
bf16 = jnp.bfloat16


def halves(table):
    high = table.astype(ml_dtypes.bfloat16)
    low = (table - high.astype(np.float64)).astype(ml_dtypes.bfloat16)
    return np.stack([high, low])


def cas(rows, columns, length):
    phase = (rows[:, None] * columns[None, :]) % length
    angle = phase * (2.0 * np.pi / length)
    return np.cos(angle) + np.sin(angle)


def z_table(length):
    index = np.arange(length)
    return halves(cas(index, index, length))


def x_tables(length):
    half = length // 2
    place = np.arange(half)
    even = cas(2 * place, place, length)
    odd = cas(2 * place + 1, place, length)
    return np.stack([halves(even), halves(odd), halves(odd.T)])


def kx_order(length):
    full = np.concatenate([np.arange(0, length, 2), np.arange(1, length, 2)])
    return np.minimum(full, length - full)


def kz_order(length):
    full = np.arange(length)
    return np.minimum(full, length - full)


def filters(tf_table, tilt_index, wedge, nx, nz):
    levels = tf_table.shape[0]
    code = jnp.where(wedge > 0, tilt_index + 1, 0).astype(bf16)
    pick_x = np.zeros((nx, tilt_index.shape[0]), ml_dtypes.bfloat16)
    pick_x[np.arange(nx), kx_order(nx)] = 1
    pick_z = np.zeros((tilt_index.shape[1], nz), ml_dtypes.bfloat16)
    pick_z[kz_order(nz), np.arange(nz)] = 1
    wide = jnp.dot(code, pick_z, preferred_element_type=f32).astype(bf16)
    spread = jnp.dot(pick_x, wide, preferred_element_type=f32)
    response = jnp.zeros_like(spread)
    for level in range(levels):
        response = jnp.where(spread == level + 1.0, tf_table[level], response)
    scale = 1.0 / (nx * nz)
    prior = scale / (response * response + 1.0)
    data = response * prior
    return data + prior, data, prior


def split(value):
    high = value.astype(bf16)
    return high, (value - high.astype(f32)).astype(bf16)


def dot3(a, b):
    dot = functools.partial(jnp.dot, preferred_element_type=f32)
    return dot(a[0], b[0]) + (dot(a[0], b[1]) + dot(a[1], b[0]))


def filter_kernel(first, halo, *refs):
    if first:
        (cells, ztab, xtab, both, data, windows, kept, waves, high, low, padded) = refs
    else:
        (cells, ztab, xtab, kept, prior, windows, waves, high, low, padded) = refs
    devices, _, slab, nz = cells.shape
    nx = devices * slab
    half = nx // 2
    tile = min(256, half)
    ztable = (ztab[0], ztab[1])
    flat = cells[:, 0].reshape(nx, nz)
    for top in range(0, half, tile):
        a = dot3(split(flat[top : top + tile]), ztable)
        b = dot3(split(flat[half + top : half + top + tile]), ztable)
        for spot, value in ((top, a + b), (half + top, a - b)):
            high[spot : spot + tile], low[spot : spot + tile] = split(value)
    for part in range(2):
        base = part * half
        folded = (high[base : base + half], low[base : base + half])
        for top in range(0, half, tile):
            rows = slice(base + top, base + top + tile)
            table = (xtab[part, 0, top : top + tile], xtab[part, 1, top : top + tile])
            wave = dot3(table, folded)
            if first:
                waves[rows] = wave * both[rows]
                kept[0, rows] = wave * data[rows]
            else:
                waves[rows] = kept[0, rows] + wave * prior[rows]
    for top in range(0, nx, tile):
        rows = slice(top, top + tile)
        high[rows], low[rows] = split(waves[rows])
    even = (high[:half], low[:half])
    odd = (high[half:], low[half:])
    padded[:SUB] = jnp.zeros((SUB, nz), f32)
    padded[halo + nx - halo % SUB : halo + nx - halo % SUB + SUB] = jnp.zeros((SUB, nz), f32)
    for top in range(0, half, tile):
        e = dot3((xtab[0, 0, top : top + tile], xtab[0, 1, top : top + tile]), even)
        o = dot3((xtab[2, 0, top : top + tile], xtab[2, 1, top : top + tile]), odd)
        padded[halo + top : halo + top + tile] = dot3(split(e + o), ztable)
        padded[halo + half + top : halo + half + top + tile] = dot3(split(e - o), ztable)
    width = slab + 2 * halo
    for device in range(devices):
        windows[device, 0] = padded[device * slab : device * slab + width]


def run_filter(first, halo, cells, tables, weights):
    devices, rows, slab, nz = cells.shape
    nx = devices * slab
    width = slab + 2 * halo
    ztab, xtab = tables

    def whole(array):
        return pl.BlockSpec(array.shape, lambda r: (0,) * array.ndim)

    def per_row(planes):
        return pl.BlockSpec((devices, 1, planes, nz), lambda r: (0, r, 0, 0))

    kept_spec = pl.BlockSpec((1, nx, nz), lambda r: (r, 0, 0))
    windows_shape = jax.ShapeDtypeStruct((devices, rows, width, nz), f32)
    kept_shape = jax.ShapeDtypeStruct((rows, nx, nz), f32)
    in_specs = [per_row(slab), whole(ztab), whole(xtab)]
    if first:
        in_specs += [whole(weights[0]), whole(weights[1])]
        out_specs, out_shape = [per_row(width), kept_spec], [windows_shape, kept_shape]
    else:
        in_specs += [kept_spec, whole(weights[1])]
        out_specs, out_shape = per_row(width), windows_shape
    flops = 3 * 2 * rows * (2 * nx * nz * nz + nx * nx * nz)
    return pl.pallas_call(
        functools.partial(filter_kernel, first, halo),
        grid=(rows,),
        in_specs=in_specs,
        out_specs=out_specs,
        out_shape=out_shape,
        scratch_shapes=[
            pltpu.VMEM((nx, nz), f32),
            pltpu.VMEM((nx, nz), bf16),
            pltpu.VMEM((nx, nz), bf16),
            pltpu.VMEM((nx + 2 * SUB, nz), f32),
        ],
        compiler_params=pltpu.CompilerParams(vmem_limit_bytes=VMEM_LIMIT),
        cost_estimate=pl.CostEstimate(
            flops=flops, bytes_accessed=8 * 1024 * 1024, transcendentals=0
        ),
    )(cells, ztab, xtab, *weights)


def lane_bends(pieces):
    lane = lax.broadcasted_iota(jnp.int32, pieces[0].shape, 1)
    up = [pltpu.roll(piece, LANE - 1, 1) for piece in pieces]
    down = [pltpu.roll(piece, 1, 1) for piece in pieces]
    bends = []
    for k, piece in enumerate(pieces):
        above = up[k + 1] if k + 1 < len(pieces) else 0.0
        below = down[k - 1] if k > 0 else 0.0
        upper = jnp.where(lane == LANE - 1, above, up[k])
        lower = jnp.where(lane == 0, below, down[k])
        bends.append(upper + lower - 2.0 * piece)
    return bends


def row_bends(groups):
    row = lax.broadcasted_iota(jnp.int32, groups[0].shape, 0)
    up = [pltpu.roll(group, SUB - 1, 0) for group in groups]
    down = [pltpu.roll(group, 1, 0) for group in groups]
    count = len(groups)
    bends = []
    for g, group in enumerate(groups):
        upper = jnp.where(row == SUB - 1, up[(g + 1) % count], up[g])
        lower = jnp.where(row == 0, down[g - 1], down[g])
        bends.append(upper + lower - 2.0 * group)
    return bends


def passes_kernel(first, last, halo, slab, nx, start_ref, target, *refs):
    if first:
        duals_in, refs = None, refs
    else:
        duals_in, refs = refs[:3], refs[3:]
    if last:
        restored, refs = refs[0], refs[1:]
    else:
        current, duals_out, refs = refs[0], refs[1:4], refs[4:]
    lead, field, dual_x, dual_y, dual_z = refs[:5]
    turned = refs[5:]
    ny, width, nz = target.shape
    groups = width // SUB
    blocks = nz // LANE
    decay = 1.0 / (1.0 + step_dual * huber_eps / bound_dual)
    gain = step_dual * decay
    origin = start_ref[0] - halo

    def inside(g):
        if SUB * g >= halo and SUB * (g + 1) <= width - halo:
            return None
        place = origin + SUB * g + lax.broadcasted_iota(jnp.int32, (SUB, LANE), 0)
        return (place >= 0) & (place < nx)

    def masked(value, g):
        mask = inside(g)
        return value if mask is None else jnp.where(mask, value, 0.0)

    def at(g, k):
        return pl.ds(SUB * g, SUB), pl.ds(LANE * k, LANE)

    empty = jnp.zeros((width, nz), f32)
    for plane in (0, ny + 1):
        lead[plane] = empty
        dual_y[plane] = empty

    @pl.loop(0, ny)
    def _(y):
        lead[y + 1] = target[y]

    for sweep in range(PASSES):
        if sweep > 0:
            before = (lambda y: (dual_x, y)), (lambda y: (dual_y, y + 1)), (lambda y: (dual_z, y))
        elif duals_in is not None:
            before = tuple((lambda y, ref=ref: (ref, y)) for ref in duals_in)
        else:
            before = None
        final = sweep == PASSES - 1

        @pl.loop(0, ny)
        def _(y):
            here = [[lead[(y + 1,) + at(g, k)] for k in range(blocks)] for g in range(groups)]
            columns = [row_bends([here[g][k] for g in range(groups)]) for k in range(blocks)]
            for g in range(groups):
                along_z = lane_bends(here[g])
                for k in range(blocks):
                    spot = at(g, k)
                    along_y = lead[(y,) + spot] + lead[(y + 2,) + spot] - 2.0 * here[g][k]
                    raised = [gain * columns[k][g], gain * along_y, gain * along_z[k]]
                    if before is not None:
                        for a in range(3):
                            ref, plane = before[a](y)
                            raised[a] = raised[a] + decay * ref[(plane,) + spot]
                    total = (
                        raised[0] * raised[0] + raised[1] * raised[1] + raised[2] * raised[2]
                    )
                    shrink = lax.rsqrt(
                        jnp.maximum(1.0, total * (1.0 / (bound_dual * bound_dual)))
                    )
                    made = [raised[0] * masked(shrink, g), raised[1] * shrink, raised[2] * shrink]
                    dual_x[(y,) + spot] = made[0]
                    dual_y[(y + 1,) + spot] = made[1]
                    dual_z[(y,) + spot] = made[2]
                    if final and not last:
                        shift = halo - HALO_LAST
                        kept_rows = slab + 2 * HALO_LAST
                        lo = max(0, shift - SUB * g)
                        hi = min(SUB, kept_rows + shift - SUB * g)
                        if lo < hi:
                            rows = pl.ds(SUB * g + lo - shift, hi - lo)
                            for a in range(3):
                                duals_out[a][y, rows, spot[1]] = made[a][lo:hi]

        @pl.loop(0, ny)
        def _(y):
            wanted = range(groups)
            if final:
                wanted = [
                    g for g in wanted if SUB * (g + 1) > halo and SUB * g < width - halo
                ]
            near = [[dual_x[(y,) + at(g, k)] for k in range(blocks)] for g in range(groups)]
            columns = [row_bends([near[g][k] for g in range(groups)]) for k in range(blocks)]
            for g in wanted:
                along_z = lane_bends([dual_z[(y,) + at(g, k)] for k in range(blocks)])
                for k in range(blocks):
                    spot = at(g, k)
                    along_y = (
                        dual_y[(y,) + spot]
                        + dual_y[(y + 2,) + spot]
                        - 2.0 * dual_y[(y + 1,) + spot]
                    )
                    adjoint = columns[k][g] + along_y + along_z[k]
                    goal = target[(y,) + spot]
                    if sweep == 0:
                        old = goal
                        updated = goal - (step_primal / (1.0 + step_primal)) * adjoint
                    else:
                        old = field[(y,) + spot]
                        updated = (old + step_primal * (goal - adjoint)) * (
                            1.0 / (1.0 + step_primal)
                        )
                    if not final:
                        field[(y,) + spot] = updated
                        lead[(y + 1,) + spot] = masked(2.0 * updated - old, g)
                        continue
                    lo = max(0, halo - SUB * g)
                    hi = min(SUB, slab + halo - SUB * g)
                    x = SUB * g + lo - halo
                    if last:
                        turned[k][pl.ds(x * ny + y, hi - lo, stride=ny), :] = updated[lo:hi]
                    else:
                        current[y, pl.ds(x, hi - lo), spot[1]] = updated[lo:hi]

    for k, block in enumerate(turned):
        restored[:, LANE * k : LANE * (k + 1)] = block[:]


def run_passes(first, last, halo, slab, start, target, duals):
    ny, width, nz = target.shape
    nx = slab * lax.axis_size("gy")
    vmem = pl.BlockSpec(memory_space=pltpu.VMEM)
    if last:
        out_shape = jax.ShapeDtypeStruct((slab * ny, nz), f32)
        out_specs = vmem
    else:
        kept = jax.ShapeDtypeStruct((ny, slab + 2 * HALO_LAST, nz), f32)
        out_shape = [jax.ShapeDtypeStruct((ny, slab, nz), f32), kept, kept, kept]
        out_specs = [vmem] * 4
    return pl.pallas_call(
        functools.partial(passes_kernel, first, last, halo, slab, nx),
        in_specs=[pl.BlockSpec(memory_space=pltpu.SMEM)] + [vmem] * (1 + len(duals)),
        out_specs=out_specs,
        out_shape=out_shape,
        scratch_shapes=[
            pltpu.VMEM((ny + 2, width, nz), f32),
            pltpu.VMEM((ny, width, nz), f32),
            pltpu.VMEM((ny, width, nz), f32),
            pltpu.VMEM((ny + 2, width, nz), f32),
            pltpu.VMEM((ny, width, nz), f32),
        ]
        + [pltpu.VMEM((slab * ny, LANE), f32)] * (nz // LANE if last else 0),
        compiler_params=pltpu.CompilerParams(vmem_limit_bytes=VMEM_LIMIT),
        cost_estimate=pl.CostEstimate(
            flops=120 * ny * width * nz,
            bytes_accessed=8 * 4 * ny * width * nz,
            transcendentals=PASSES * ny * width * nz,
        ),
    )(start, target, *duals)


def exchange(blocks):
    return lax.all_to_all(blocks, "gy", split_axis=0, concat_axis=0, tiled=True)


def local(observed, tf_table, tilt_index, wedge):
    slab, ny, nz = observed.shape
    devices = lax.axis_size("gy")
    rows = ny // devices
    nx = slab * devices
    start = (lax.axis_index("gy") * slab).astype(jnp.int32).reshape(1)
    tables = (jnp.asarray(z_table(nz)), jnp.asarray(x_tables(nx)))
    cells = exchange(observed.transpose(1, 0, 2).reshape(devices, rows, slab, nz))
    both, data, prior = filters(tf_table, tilt_index, wedge, nx, nz)
    duals = ()
    for outer in range(OUTER):
        first, last = outer == 0, outer == OUTER - 1
        halo = HALO_LAST if last else HALO_FIRST
        if first:
            windows, kept = run_filter(True, halo, cells, tables, (both, data))
        else:
            windows = run_filter(False, halo, cells, tables, (kept, prior))
        target = exchange(windows).reshape(ny, slab + 2 * halo, nz)
        made = run_passes(first, last, halo, slab, start, target, duals)
        if last:
            return made.reshape(slab, ny, nz)
        duals = tuple(made[1:])
        cells = exchange(made[0].reshape(devices, rows, slab, nz))


def solution(mesh):
    in_specs = (P(("groups", "gy"), None, None), P(), P(), P())
    out_specs = P(("groups", "gy"), None, None)
    return jax.shard_map(local, mesh=mesh, in_specs=in_specs, out_specs=out_specs, check_vma=False)
```

time: 308 us -> 167 us (0.54)
  matrix products: 103 us -> 14.7 us
  starting transfers between devices: 48 us -> 12 us
  waiting for transfers between devices: 72.9 us -> 38.3 us
  Pallas kernels: 0 us -> 27.9 us
  other arithmetic: 14.8 us -> 0 us
  blocking collectives: 60.1 us -> 63.9 us
    dot_general x12 -> x1, matrix products: 103 us -> 14.7 us  [filters(): spread = jnp.dot(pick_x, wide, preferred_element_type=f32)]
    ppermute x16 -> x0, starting transfers between devices: 35.5 us -> none  [the longest x8 18.6 us: extended(): before = lax.ppermute(last, axis, up)]
    pallas_call x0 -> x4, Pallas kernels: none -> 27.9 us  [the longest x2 17.1 us: run_passes(): pl.pallas_call(functools.partial(passes_kernel, first, last, halo, slab,...]
    ppermute x16 -> x0, waiting for transfers between devices: 26.8 us -> none  [the longest x8 26.8 us: extended(): before = lax.ppermute(last, axis, up)]
    div x12 -> x0, other arithmetic: 11 us -> none  [the longest x8 8.02 us: denoise(): duals = (raised[0] / shrink, raised[1] / shrink, raised[2] / shrink)]
    all_to_all x2, waiting for transfers between devices: 46.1 us -> 38.3 us  [exchange(): return lax.all_to_all(blocks, 'gy', split_axis=0, concat_axis=0, tiled=True)]
    unnamed x14 -> x19, local copies, waits for them, and re-layouts: 1.36 us -> 6.25 us
    all_to_all x2, blocking collectives: 60.1 us -> 63.9 us  [exchange(): return lax.all_to_all(blocks, 'gy', split_axis=0, concat_axis=0, tiled=True)]
  transfers between devices with their start and end apart: 18 -> 2, of which waited for: 10 -> 2; matrix products, arithmetic and copies ran while one was open for 1% -> 9% of each run, Pallas kernels for 0% -> 0%
where the time goes in v1:
time: 167 us; the launch traced here: 164 us
  blocking collectives  63.9 us (38%)
  waiting for transfers between devices  38.3 us (23%)
  Pallas kernels  27.9 us (17%)
  matrix products  14.7 us (9%)
  starting transfers between devices  12 us (7%)
  local copies, waits for them, and re-layouts  6.97 us (4%)
    all_to_all x2, blocking collectives, exchange(): return lax.all_to_all(blocks, 'gy', split_axis=0, concat_axis=0, tiled=True)  63.9 us
    all_to_all x2, waiting for transfers between devices, exchange(): return lax.all_to_all(blocks, 'gy', split_axis=0, concat_axis=0, tiled=True)  38.3 us
    pallas_call x2, Pallas kernels, run_passes(): pl.pallas_call(functools.partial(passes_kernel, first, last, halo, slab,...  17.1 us
    dot_general x1, matrix products, filters(): spread = jnp.dot(pick_x, wide, preferred_element_type=f32)  14.7 us
    all_to_all x2, starting transfers between devices, exchange(): return lax.all_to_all(blocks, 'gy', split_axis=0, concat_axis=0, tiled=True)  12 us
    pallas_call x2, Pallas kernels, run_filter(): pl.pallas_call(functools.partial(filter_kernel, first, halo), grid=(rows,...  10.8 us
    unnamed x19, local copies, waits for them, and re-layouts  6.25 us
  transfers between devices with their start and end apart: 2, of which 2 were waited for; matrix products, arithmetic and copies ran while one was open for 9% of the time, Pallas kernels for 0%

profile of v1, /device:TPU:8, one launch (start us, length us, event | category | flops | bytes accessed | tf_op | source)
XLA Modules:
  0.0 163.9 jit_solution(1563310359446753139)
XLA Ops:
  0.0 2.8 %copy.47 = f32[64,16,256]{2,0,1:T(8,128)} copy(f32[64,16,256]{2,1,0:T(8,128)} %param.8) | data formatting | bytes 2097152 | tf_op args[0]
  2.8 0.0 copy-start.5
  2.8 0.0 copy-start.6
  2.8 0.0 copy-start.7
  2.8 0.0 copy-start.8
  2.8 6.4 %all-to-all-start = ((f32[16,1,64,256]{3,2,1,0:T(8,128)}), f32[16,1,64,256]{3,2,1,0:T(8,128)S(1)}, u32[]{:S(2)}, u32[]{:S(2)}) async-start(f32[16,1,64,256]{3,2,1,0:T(8,128)} %bitcast.31), calls=%async_computation | async-start | bytes 2097152 | tf_op jit(solution)/shard_map/all_to_all | solution.py:368
  9.3 0.0 copy-done.5
  9.3 0.7 fusion.11
  10.0 0.0 copy-done.6
  10.0 0.0 copy-done.7
  10.0 0.0 copy-done.8
  10.0 0.0 copy-start
  10.0 14.7 %add_divide_fusion = (f32[1024,256]{1,0:T(8,128)S(1)}, f32[1024,256]{1,0:T(8,128)}, f32[1024,256]{1,0:T(8,128)}) fusion(f32[]{:T(128)} %bitcast.19, f32[]{:T(128)} %bitcast.18, f32[]{:T(128)} %bitcast.17, f32[]{:T(128)} %bitcast.16, f32[]{:T(128)} %bitcast.15, f32[]{:T(128)} %bitcast.14, f32[]{:T(128)} %bitcast.13, f32[]{:T(128)} %bitcast.12, f32[]{:T(128)} %bitcast.11, ...), kind=kOutput, calls=%fused_computation.4 | convolution fusion | flops 312937728 | bytes 4791880 | tf_op jit(solution)/shard_map/dot_general | solution.py:73
  24.7 8.7 %all-to-all-done.refs_0_ = f32[16,1,64,256]{3,2,1,0:T(8,128)S(1)} async-done(((f32[16,1,64,256]{3,2,1,0:T(8,128)}), f32[16,1,64,256]{3,2,1,0:T(8,128)S(1)}, u32[]{:S(2)}, u32[]{:S(2)}) %all-to-all-start) | async-done | bytes 1048608 | tf_op jit(solution)/shard_map/all_to_all | solution.py:368
  33.5 0.0 copy-done
  33.5 0.0 copy-start.3
  33.5 1.2 copy-done.3
  34.7 0.0 copy-start.4
  34.7 1.2 copy-done.4
  35.9 6.0 %shard_map.82 = (f32[16,1,80,256]{3,2,1,0:T(8,128)}, f32[1,1024,256]{2,1,0:T(8,128)S(1)}) custom-call(f32[16,1,64,256]{3,2,1,0:T(8,128)S(1)} %all-to-all-done.refs_0_, bf16[2,256,256]{2,1,0:T(8,128)(2,1)S(1)} %copy-done, bf16[3,2,512,512]{3,2,1,0:T(8,128)(2,1)} %constant.56.clone.refs_2_, f32[1024,256]{1,0:T(8,128)S(1)} %copy-done.3, f32[1024,256]{1,0:T(8,128)S(1)} %copy-done.4), custom_call_target="tpu_custom_call" | custom-call | flops 2415919104 | bytes 8388608 | tf_op jit(solution)/shard_map/pallas_call | solution.py:161
  41.9 0.0 copy-start.1
  41.9 1.0 copy-done.1
  42.9 5.6 %all-to-all-start.1 = ((f32[16,1,80,256]{3,2,1,0:T(8,128)}), f32[16,1,80,256]{3,2,1,0:T(8,128)S(1)}, u32[]{:S(2)}, u32[]{:S(2)}) async-start(f32[16,1,80,256]{3,2,1,0:T(8,128)} %get-tuple-element.11), calls=%async_computation.1 | async-start | bytes 2621440 | tf_op jit(solution)/shard_map/all_to_all | solution.py:368
  48.4 29.6 %all-to-all-done.1 = f32[16,1,80,256]{3,2,1,0:T(8,128)S(1)} async-done(((f32[16,1,80,256]{3,2,1,0:T(8,128)}), f32[16,1,80,256]{3,2,1,0:T(8,128)S(1)}, u32[]{:S(2)}, u32[]{:S(2)}) %all-to-all-start.1) | async-done | bytes 1310752 | tf_op jit(solution)/shard_map/all_to_all | solution.py:368
  78.0 8.0 %shard_map.83 = (f32[16,64,256]{2,1,0:T(8,128)S(1)}, f32[16,72,256]{2,1,0:T(8,128)S(1)}, f32[16,72,256]{2,1,0:T(8,128)S(1)}, f32[16,72,256]{2,1,0:T(8,128)S(1)}) custom-call(s32[1]{0:T(128)} %bitcast.start_ref, f32[16,80,256]{2,1,0:T(8,128)S(1)} %bitcast.32), custom_call_target="tpu_custom_call" | custom-call | flops 39321600 | bytes 10485760 | tf_op jit(solution)/shard_map/pallas_call | solution.py:345
  86.0 0.0 copy-start.2
  86.0 30.7 %all_to_all.20.refs_0_ = f32[16,1,64,256]{3,2,1,0:T(8,128)S(1)} all-to-all(f32[16,1,64,256]{3,2,1,0:T(8,128)S(1)} %bitcast.34), channel_id=1, replica_groups=mesh['groups'=2,'gy'=16] {'gy'}, dimensions={0} | all-to-all | bytes 2097152 | tf_op jit(solution)/shard_map/all_to_all | solution.py:368
  116.7 0.0 copy-done.2
  116.7 4.9 %shard_map.84 = f32[16,1,72,256]{3,2,1,0:T(8,128)S(1)} custom-call(f32[16,1,64,256]{3,2,1,0:T(8,128)S(1)} %all_to_all.20.refs_0_, bf16[2,256,256]{2,1,0:T(8,128)(2,1)S(1)} %copy-done, bf16[3,2,512,512]{3,2,1,0:T(8,128)(2,1)} %constant.56.clone.refs_2_, f32[1,1024,256]{2,1,0:T(8,128)S(1)} %copy-done.2, f32[1024,256]{1,0:T(8,128)S(1)} %get-tuple-element.17.refs_4_), custom_call_target="tpu_custom_call" | custom-call | flops 2415919104 | bytes 8388608 | tf_op jit(solution)/shard_map/pallas_call | solution.py:161
  121.6 33.2 %all_to_all.21 = f32[16,1,72,256]{3,2,1,0:T(8,128)S(1)} all-to-all(f32[16,1,72,256]{3,2,1,0:T(8,128)S(1)} %shard_map.84), channel_id=1, replica_groups=mesh['groups'=2,'gy'=16] {'gy'}, dimensions={0} | all-to-all | bytes 2359296 | tf_op jit(solution)/shard_map/all_to_all | solution.py:368
  154.8 9.1 %shard_map.85 = f32[1024,256]{1,0:T(8,128)} custom-call(s32[1]{0:T(128)} %bitcast.start_ref, f32[16,72,256]{2,1,0:T(8,128)S(1)} %bitcast.33, f32[16,72,256]{2,1,0:T(8,128)S(1)} %get-tuple-element.14.refs_0_, f32[16,72,256]{2,1,0:T(8,128)S(1)} %get-tuple-element.15.refs_1_, f32[16,72,256]{2,1,0:T(8,128)S(1)} %get-tuple-element.16.refs_2_), custom_call_target="tpu_custom_call" | custom-call | flops 35389440 | bytes 9437184 | tf_op jit(solution)/shard_map/pallas_call | solution.py:345
Async XLA Ops:
  2.8 6.5 %copy-start.5 = (f32[16]{0:T(128)S(1)}, f32[16]{0:T(128)}, u32[]{:S(2)}) copy-start(f32[16]{0:T(128)} %param.9) | copy-start | bytes 196
  2.8 7.2 %copy-start.6 = (s32[513,129]{0,1:T(8,128)S(1)}, s32[513,129]{0,1:T(8,128)}, u32[]{:S(2)}) copy-start(s32[513,129]{0,1:T(8,128)} %param.10) | copy-start | bytes 794128
  2.8 7.2 %copy-start.7 = (s32[513,129]{0,1:T(8,128)S(1)}, s32[513,129]{0,1:T(8,128)}, u32[]{:S(2)}) copy-start(s32[513,129]{0,1:T(8,128)} %param.11) | copy-start | bytes 794128
  2.8 7.2 %copy-start.8 = (bf16[129,256]{1,0:T(8,128)(2,1)S(1)}, bf16[129,256]{1,0:T(8,128)(2,1)}, u32[]{:S(2)}) copy-start(bf16[129,256]{1,0:T(8,128)(2,1)} %constant.57.clone) | copy-start | bytes 198148
  2.8 30.7 %all-to-all-start = ((f32[16,1,64,256]{3,2,1,0:T(8,128)}), f32[16,1,64,256]{3,2,1,0:T(8,128)S(1)}, u32[]{:S(2)}, u32[]{:S(2)}) async-start(f32[16,1,64,256]{3,2,1,0:T(8,128)} %bitcast.31), calls=%async_computation | async-start | bytes 2097152 | tf_op jit(solution)/shard_map/all_to_all | solution.py:368
  10.0 23.5 %copy-start = (bf16[2,256,256]{2,1,0:T(8,128)(2,1)S(1)}, bf16[2,256,256]{2,1,0:T(8,128)(2,1)}, u32[]{:S(2)}) copy-start(bf16[2,256,256]{2,1,0:T(8,128)(2,1)} %constant.25.clone.refs_1_) | copy-start | bytes 786436
  33.5 1.2 copy-start.3
  34.7 1.2 copy-start.4
  41.9 1.0 copy-start.1
  42.9 35.1 %all-to-all-start.1 = ((f32[16,1,80,256]{3,2,1,0:T(8,128)}), f32[16,1,80,256]{3,2,1,0:T(8,128)S(1)}, u32[]{:S(2)}, u32[]{:S(2)}) async-start(f32[16,1,80,256]{3,2,1,0:T(8,128)} %get-tuple-element.11), calls=%async_computation.1 | async-start | bytes 2621440 | tf_op jit(solution)/shard_map/all_to_all | solution.py:368
  86.0 30.7 %copy-start.2 = (f32[1,1024,256]{2,1,0:T(8,128)S(1)}, f32[1,1024,256]{2,1,0:T(8,128)}, u32[]{:S(2)}) copy-start(f32[1,1024,256]{2,1,0:T(8,128)} %copy-done.1) | copy-start | bytes 3145732

commit v2 on v1

v2 whole, which is shorter than its diff:
```python
import functools

import jax
import jax.numpy as jnp
import ml_dtypes
import numpy as np
from jax import lax
from jax.experimental import pallas as pl
from jax.experimental.pallas import tpu as pltpu
from jax.sharding import PartitionSpec as P

OUTER = 2
PASSES = 2

step_dual = 0.14
step_primal = 0.14
huber_eps = 0.05
bound_dual = 0.5

SUB = 8
LANE = 128
HALO_LAST = 4
HALO_FIRST = 8
MIB = 1024 * 1024

f32 = jnp.float32
bf16 = jnp.bfloat16


def halves(table):
    high = table.astype(ml_dtypes.bfloat16)
    low = (table - high.astype(np.float64)).astype(ml_dtypes.bfloat16)
    return np.stack([high, low])


def cas(rows, columns, length):
    phase = (rows[:, None] * columns[None, :]) % length
    angle = phase * (2.0 * np.pi / length)
    return np.cos(angle) + np.sin(angle)


def z_table(length):
    index = np.arange(length)
    return halves(cas(index, index, length))


def x_tables(length, slab, chunks):
    half = length // 2
    place = np.arange(half)
    forward = []
    for chunk in range(chunks):
        cells = place[place % slab // (slab // chunks) == chunk]
        forward.append(
            np.stack(
                [halves(cas(2 * place, cells, length)), halves(cas(2 * place + 1, cells, length))]
            )
        )
    inverse = np.stack(
        [halves(cas(place, 2 * place, length)), halves(cas(place, 2 * place + 1, length))]
    )
    return forward, inverse


def padded_to(length, unit):
    return -(-length // unit) * unit


def weights_kernel(nx, nz, levels, table_ref, code_ref, both, data, prior):
    half = nx // 2
    tile = min(256, half)
    heights, widths = code_ref.shape
    scale = 1.0 / (nx * nz)
    kz = lax.broadcasted_iota(jnp.int32, (heights, nz), 1)
    kz = jnp.minimum(kz, nz - kz)
    pick_z = jnp.where(kz == lax.broadcasted_iota(jnp.int32, (heights, nz), 0), 1.0, 0.0)
    pick_z = pick_z.astype(bf16)
    for part in range(2):
        for top in range(0, half, tile):
            kx = 2 * (top + lax.broadcasted_iota(jnp.int32, (tile, widths), 0)) + part
            kx = jnp.minimum(kx, nx - kx)
            pick_x = jnp.where(kx == lax.broadcasted_iota(jnp.int32, (tile, widths), 1), 1.0, 0.0)
            tall = lax.dot_general(
                pick_x.astype(bf16),
                code_ref[...],
                (((1,), (1,)), ((), ())),
                preferred_element_type=f32,
            )
            spread = jnp.dot(tall.astype(bf16), pick_z, preferred_element_type=f32)
            response = jnp.zeros_like(spread)
            for level in range(levels):
                response = jnp.where(spread == level + 1.0, table_ref[level], response)
            gain = scale / (response * response + 1.0)
            rows = slice(part * half + top, part * half + top + tile)
            prior[rows] = gain
            data[rows] = response * gain
            both[rows] = response * gain + gain


def make_weights(tf_table, tilt_index, wedge, nx, nz):
    levels = tf_table.shape[0]
    code = jnp.where(wedge > 0, tilt_index + 1, 0).T
    extra = [(0, padded_to(size, LANE) - size) for size in code.shape]
    code = jnp.pad(code, extra).astype(bf16)
    grid = jax.ShapeDtypeStruct((nx, nz), f32)
    vmem = pl.BlockSpec(memory_space=pltpu.VMEM)
    return pl.pallas_call(
        functools.partial(weights_kernel, nx, nz, levels),
        in_specs=[pl.BlockSpec(memory_space=pltpu.SMEM), vmem],
        out_specs=[vmem] * 3,
        out_shape=[grid] * 3,
        compiler_params=pltpu.CompilerParams(vmem_limit_bytes=16 * MIB),
        cost_estimate=pl.CostEstimate(
            flops=60 * nx * nz, bytes_accessed=12 * nx * nz, transcendentals=0
        ),
    )(tf_table, code)


def split(value):
    high = value.astype(bf16)
    return high, (value - high.astype(f32)).astype(bf16)


def dot3(a, b):
    dot = functools.partial(jnp.dot, preferred_element_type=f32)
    return dot(a[0], b[0]) + (dot(a[0], b[1]) + dot(a[1], b[0]))


def filter_kernel(first, opens, closes, halo, slab, *refs):
    cells, ztab, forward, refs = refs[0], refs[1], refs[2], refs[3:]
    if not opens:
        so_far, refs = refs[0], refs[1:]
    if closes:
        inverse, refs = refs[0], refs[1:]
        if first:
            both, data, refs = refs[0], refs[1], refs[2:]
        else:
            kept, prior, refs = refs[0], refs[1], refs[2:]
        count = len(refs) - (6 if first else 5)
        windows, refs = refs[:count], refs[count:]
        if first:
            kept, refs = refs[0], refs[1:]
        high, low, wave_high, wave_low, padded = refs
    else:
        sums, high, low = refs
    devices, rows, chunk, nz = cells.shape
    nx = devices * slab
    half = nx // 2
    folds = devices * chunk // 2
    ztable = (ztab[0], ztab[1])
    for r in range(rows):
        flat = cells[:, r].reshape(2 * folds, nz)
        tile = min(256, folds)
        for top in range(0, folds, tile):
            a = dot3(split(flat[top : top + tile]), ztable)
            b = dot3(split(flat[folds + top : folds + top + tile]), ztable)
            for spot, value in ((top, a + b), (folds + top, a - b)):
                high[spot : spot + tile], low[spot : spot + tile] = split(value)
        tile = min(256, half)
        for part in range(2):
            base = part * folds
            folded = (high[base : base + folds], low[base : base + folds])
            for top in range(0, half, tile):
                spot = slice(part * half + top, part * half + top + tile)
                table = (forward[part, 0, top : top + tile], forward[part, 1, top : top + tile])
                wave = dot3(table, folded)
                if not opens:
                    wave = so_far[r, spot] + wave
                if not closes:
                    sums[r, spot] = wave
                    continue
                if first:
                    mixed = wave * both[spot]
                    kept[r, spot] = wave * data[spot]
                else:
                    mixed = kept[r, spot] + wave * prior[spot]
                wave_high[spot], wave_low[spot] = split(mixed)
        if not closes:
            continue
        even = (wave_high[:half], wave_low[:half])
        odd = (wave_high[half:], wave_low[half:])
        after = halo + nx - halo % SUB
        padded[:SUB] = jnp.zeros((SUB, nz), f32)
        padded[after : after + SUB] = jnp.zeros((SUB, nz), f32)
        for top in range(0, half, tile):
            e = dot3((inverse[0, 0, top : top + tile], inverse[0, 1, top : top + tile]), even)
            o = dot3((inverse[1, 0, top : top + tile], inverse[1, 1, top : top + tile]), odd)
            padded[halo + top : halo + top + tile] = dot3(split(e + o), ztable)
            padded[halo + half + top : halo + half + top + tile] = dot3(split(e - o), ztable)
        for device in range(devices):
            spot = device * slab
            for window in windows:
                width = window.shape[2]
                window[device, r] = padded[spot : spot + width]
                spot += width


def start_filter(cells, tables, chunk, slab):
    devices, rows, size, nz = cells.shape
    nx = devices * slab
    ztab, forward, _ = tables
    vmem = pl.BlockSpec(memory_space=pltpu.VMEM)
    folds = devices * size
    return pl.pallas_call(
        functools.partial(filter_kernel, False, True, False, 0, slab),
        in_specs=[vmem] * 3,
        out_specs=vmem,
        out_shape=jax.ShapeDtypeStruct((rows, nx, nz), f32),
        scratch_shapes=[pltpu.VMEM((folds, nz), bf16), pltpu.VMEM((folds, nz), bf16)],
        compiler_params=pltpu.CompilerParams(vmem_limit_bytes=16 * MIB),
        cost_estimate=pl.CostEstimate(
            flops=6 * rows * folds * nz * (nz + nx // 2),
            bytes_accessed=4 * rows * nx * nz,
            transcendentals=0,
        ),
    )(cells, ztab, forward[chunk])


def finish_filter(first, halo, cells, so_far, tables, weights, chunk, slab, widths):
    devices, rows, size, nz = cells.shape
    nx = devices * slab
    ztab, forward, inverse = tables
    vmem = pl.BlockSpec(memory_space=pltpu.VMEM)
    folds = devices * size
    operands = [cells, ztab, forward[chunk]] + so_far + [inverse] + list(weights)
    out_shape = [jax.ShapeDtypeStruct((devices, rows, width, nz), f32) for width in widths]
    if first:
        out_shape.append(jax.ShapeDtypeStruct((rows, nx, nz), f32))
    return pl.pallas_call(
        functools.partial(filter_kernel, first, not so_far, True, halo, slab),
        in_specs=[vmem] * len(operands),
        out_specs=[vmem] * len(out_shape),
        out_shape=out_shape,
        scratch_shapes=[
            pltpu.VMEM((folds, nz), bf16),
            pltpu.VMEM((folds, nz), bf16),
            pltpu.VMEM((nx, nz), bf16),
            pltpu.VMEM((nx, nz), bf16),
            pltpu.VMEM((nx + 2 * SUB, nz), f32),
        ],
        compiler_params=pltpu.CompilerParams(vmem_limit_bytes=24 * MIB),
        cost_estimate=pl.CostEstimate(
            flops=6 * rows * nx * nz * (2 * nz + nx),
            bytes_accessed=8 * rows * nx * nz,
            transcendentals=0,
        ),
    )(*operands)


def lane_bends(pieces):
    lane = lax.broadcasted_iota(jnp.int32, pieces[0].shape, 1)
    up = [pltpu.roll(piece, LANE - 1, 1) for piece in pieces]
    down = [pltpu.roll(piece, 1, 1) for piece in pieces]
    bends = []
    for k, piece in enumerate(pieces):
        above = up[k + 1] if k + 1 < len(pieces) else 0.0
        below = down[k - 1] if k > 0 else 0.0
        upper = jnp.where(lane == LANE - 1, above, up[k])
        lower = jnp.where(lane == 0, below, down[k])
        bends.append(upper + lower - 2.0 * piece)
    return bends


def row_bends(groups):
    row = lax.broadcasted_iota(jnp.int32, groups[0].shape, 0)
    up = [pltpu.roll(group, SUB - 1, 0) for group in groups]
    down = [pltpu.roll(group, 1, 0) for group in groups]
    count = len(groups)
    bends = []
    for g, group in enumerate(groups):
        upper = jnp.where(row == SUB - 1, up[(g + 1) % count], up[g])
        lower = jnp.where(row == 0, down[g - 1], down[g])
        bends.append(upper + lower - 2.0 * group)
    return bends


def passes_kernel(first, last, chunk, halo, slab, nx, start_ref, *refs):
    pieces, refs = refs[: min(chunk, 1) + 1], refs[min(chunk, 1) + 1 :]
    if first:
        duals_in, refs = None, refs
    else:
        duals_in, refs = refs[:3], refs[3:]
    if last and chunk:
        before_this, refs = refs[:chunk], refs[chunk:]
    if last:
        restored, refs = refs[0], refs[1:]
    else:
        current, duals_out, refs = refs[0], refs[1:4], refs[4:]
    lead, field, dual_x, dual_y, dual_z = refs[:5]
    turned = refs[5:]
    ny, _, nz = pieces[0].shape
    width = slab + 2 * halo
    groups = width // SUB
    blocks = nz // LANE
    decay = 1.0 / (1.0 + step_dual * huber_eps / bound_dual)
    gain = step_dual * decay
    origin = start_ref[0] + chunk * slab - halo
    shared = 2 * halo if chunk else 0

    def goal_of(y, g, k):
        lanes = pl.ds(LANE * k, LANE)
        if SUB * g < shared:
            return pieces[0][y, pl.ds(pieces[0].shape[1] - shared + SUB * g, SUB), lanes]
        return pieces[-1][y, pl.ds(SUB * g - shared, SUB), lanes]

    def inside(g):
        if SUB * g >= halo and SUB * (g + 1) <= width - halo:
            return None
        place = origin + SUB * g + lax.broadcasted_iota(jnp.int32, (SUB, LANE), 0)
        return (place >= 0) & (place < nx)

    def masked(value, g):
        mask = inside(g)
        return value if mask is None else jnp.where(mask, value, 0.0)

    def at(g, k):
        return pl.ds(SUB * g, SUB), pl.ds(LANE * k, LANE)

    empty = jnp.zeros((width, nz), f32)
    for plane in (0, ny + 1):
        lead[plane] = empty
        dual_y[plane] = empty

    @pl.loop(0, ny)
    def _(y):
        if shared:
            lead[y + 1, :shared] = pieces[0][y, pieces[0].shape[1] - shared :]
        lead[y + 1, shared:] = pieces[-1][y]

    for sweep in range(PASSES):
        if sweep > 0:
            before = (lambda y: (dual_x, y)), (lambda y: (dual_y, y + 1)), (lambda y: (dual_z, y))
        elif duals_in is not None:
            before = tuple((lambda y, ref=ref: (ref, y)) for ref in duals_in)
        else:
            before = None
        final = sweep == PASSES - 1

        @pl.loop(0, ny)
        def _(y):
            here = [[lead[(y + 1,) + at(g, k)] for k in range(blocks)] for g in range(groups)]
            columns = [row_bends([here[g][k] for g in range(groups)]) for k in range(blocks)]
            for g in range(groups):
                along_z = lane_bends(here[g])
                for k in range(blocks):
                    spot = at(g, k)
                    along_y = lead[(y,) + spot] + lead[(y + 2,) + spot] - 2.0 * here[g][k]
                    raised = [gain * columns[k][g], gain * along_y, gain * along_z[k]]
                    if before is not None:
                        for a in range(3):
                            ref, plane = before[a](y)
                            raised[a] = raised[a] + decay * ref[(plane,) + spot]
                    total = (
                        raised[0] * raised[0] + raised[1] * raised[1] + raised[2] * raised[2]
                    )
                    shrink = lax.rsqrt(
                        jnp.maximum(1.0, total * (1.0 / (bound_dual * bound_dual)))
                    )
                    made = [raised[0] * masked(shrink, g), raised[1] * shrink, raised[2] * shrink]
                    dual_x[(y,) + spot] = made[0]
                    dual_y[(y + 1,) + spot] = made[1]
                    dual_z[(y,) + spot] = made[2]
                    if final and not last:
                        shift = halo - HALO_LAST
                        kept_rows = slab + 2 * HALO_LAST
                        lo = max(0, shift - SUB * g)
                        hi = min(SUB, kept_rows + shift - SUB * g)
                        if lo < hi:
                            rows = pl.ds(SUB * g + lo - shift, hi - lo)
                            for a in range(3):
                                duals_out[a][y, rows, spot[1]] = made[a][lo:hi]

        @pl.loop(0, ny)
        def _(y):
            wanted = range(groups)
            if final:
                wanted = [
                    g for g in wanted if SUB * (g + 1) > halo and SUB * g < width - halo
                ]
            near = [[dual_x[(y,) + at(g, k)] for k in range(blocks)] for g in range(groups)]
            columns = [row_bends([near[g][k] for g in range(groups)]) for k in range(blocks)]
            for g in wanted:
                along_z = lane_bends([dual_z[(y,) + at(g, k)] for k in range(blocks)])
                for k in range(blocks):
                    spot = at(g, k)
                    along_y = (
                        dual_y[(y,) + spot]
                        + dual_y[(y + 2,) + spot]
                        - 2.0 * dual_y[(y + 1,) + spot]
                    )
                    adjoint = columns[k][g] + along_y + along_z[k]
                    goal = goal_of(y, g, k)
                    if sweep == 0:
                        old = goal
                        updated = goal - (step_primal / (1.0 + step_primal)) * adjoint
                    else:
                        old = field[(y,) + spot]
                        updated = (old + step_primal * (goal - adjoint)) * (
                            1.0 / (1.0 + step_primal)
                        )
                    if not final:
                        field[(y,) + spot] = updated
                        lead[(y + 1,) + spot] = masked(2.0 * updated - old, g)
                        continue
                    lo = max(0, halo - SUB * g)
                    hi = min(SUB, slab + halo - SUB * g)
                    x = SUB * g + lo - halo
                    if last:
                        turned[k][pl.ds(x * ny + y, hi - lo, stride=ny), :] = updated[lo:hi]
                    else:
                        current[y, pl.ds(x, hi - lo), spot[1]] = updated[lo:hi]

    if last:
        for c in range(chunk):
            restored[c * slab * ny : (c + 1) * slab * ny] = before_this[c][:]
        base = chunk * slab * ny
        for k, block in enumerate(turned):
            restored[base:, LANE * k : LANE * (k + 1)] = block[:]


def run_passes(first, last, chunk, halo, slab, nx, start, pieces, duals, done):
    ny, _, nz = pieces[0].shape
    width = slab + 2 * halo
    vmem = pl.BlockSpec(memory_space=pltpu.VMEM)
    if last:
        out_shape = jax.ShapeDtypeStruct(((chunk + 1) * slab * ny, nz), f32)
        out_specs = vmem
    else:
        kept = jax.ShapeDtypeStruct((ny, slab + 2 * HALO_LAST, nz), f32)
        out_shape = [jax.ShapeDtypeStruct((ny, slab, nz), f32), kept, kept, kept]
        out_specs = [vmem] * 4
    operands = list(pieces) + list(duals) + list(done)
    field = ny * padded_to(width, SUB) * nz * 4
    return pl.pallas_call(
        functools.partial(passes_kernel, first, last, chunk, halo, slab, nx),
        in_specs=[pl.BlockSpec(memory_space=pltpu.SMEM)] + [vmem] * len(operands),
        out_specs=out_specs,
        out_shape=out_shape,
        scratch_shapes=[
            pltpu.VMEM((ny + 2, width, nz), f32),
            pltpu.VMEM((ny, width, nz), f32),
            pltpu.VMEM((ny, width, nz), f32),
            pltpu.VMEM((ny + 2, width, nz), f32),
            pltpu.VMEM((ny, width, nz), f32),
        ]
        + [pltpu.VMEM((slab * ny, LANE), f32)] * (nz // LANE if last else 0),
        compiler_params=pltpu.CompilerParams(vmem_limit_bytes=12 * field + 8 * MIB),
        cost_estimate=pl.CostEstimate(
            flops=60 * PASSES * ny * width * nz,
            bytes_accessed=8 * 4 * ny * width * nz,
            transcendentals=PASSES * ny * width * nz,
        ),
    )(start, *operands)


def exchange(blocks):
    return lax.all_to_all(blocks, "gy", split_axis=0, concat_axis=0, tiled=True)


def local(observed, tf_table, tilt_index, wedge):
    slab, ny, nz = observed.shape
    devices = lax.axis_size("gy")
    rows = ny // devices
    nx = slab * devices
    chunks = 2 if slab % (2 * SUB) == 0 and slab >= 4 * HALO_FIRST else 1
    size = slab // chunks
    start = (lax.axis_index("gy") * slab).astype(jnp.int32).reshape(1)
    forward, inverse = x_tables(nx, slab, chunks)
    tables = (
        jnp.asarray(z_table(nz)),
        [jnp.asarray(table) for table in forward],
        jnp.asarray(inverse),
    )
    cells = []
    for chunk in range(chunks):
        part = lax.slice_in_dim(observed, chunk * size, (chunk + 1) * size, axis=0)
        cells.append(exchange(part.transpose(1, 0, 2).reshape(devices, rows, size, nz)))
    both, data, prior = make_weights(tf_table, tilt_index, wedge, nx, nz)
    duals = [()] * chunks
    for outer in range(OUTER):
        first, last = outer == 0, outer == OUTER - 1
        halo = HALO_LAST if last else HALO_FIRST
        so_far = [start_filter(cells[0], tables, 0, slab)] if chunks > 1 else []
        weights = (both, data) if first else (kept, prior)
        widths = [size + 2 * halo] + [size] * (chunks - 1)
        made = finish_filter(
            first, halo, cells[-1], so_far, tables, weights, chunks - 1, slab, widths
        )
        if first:
            kept = made[chunks]
        pieces = [
            exchange(made[chunk]).reshape(ny, widths[chunk], nz) for chunk in range(chunks)
        ]
        cells, done = [], []
        for chunk in range(chunks):
            used = pieces[max(chunk - 1, 0) : chunk + 1]
            out = run_passes(
                first, last, chunk, halo, size, nx, start, used, duals[chunk], done
            )
            if last:
                done = [out]
                continue
            duals[chunk] = tuple(out[1:])
            cells.append(exchange(out[0].reshape(devices, rows, size, nz)))
    return done[0].reshape(slab, ny, nz)


def solution(mesh):
    in_specs = (P(("groups", "gy"), None, None), P(), P(), P())
    out_specs = P(("groups", "gy"), None, None)
    return jax.shard_map(local, mesh=mesh, in_specs=in_specs, out_specs=out_specs, check_vma=False)
```

time: 167 us -> 191 us (1.14)
  local copies, waits for them, and re-layouts: 6.97 us -> 30.2 us
  starting transfers between devices: 12 us -> 30.5 us
  blocking collectives: 63.9 us -> 46.2 us
  matrix products: 14.7 us -> 0 us
  Pallas kernels: 27.9 us -> 39.3 us
  waiting for transfers between devices: 38.3 us -> 41.7 us
    unnamed x19 -> x68, local copies, waits for them, and re-layouts: 6.25 us -> 28.9 us
    all_to_all x2 -> x6, starting transfers between devices: 12 us -> 30.5 us  [exchange(): return lax.all_to_all(blocks, 'gy', split_axis=0, concat_axis=0, tiled=True)]
    all_to_all x2, blocking collectives: 63.9 us -> 46.2 us  [exchange(): return lax.all_to_all(blocks, 'gy', split_axis=0, concat_axis=0, tiled=True)]
    dot_general x1 -> x0, matrix products: 14.7 us -> none  [filters(): spread = jnp.dot(pick_x, wide, preferred_element_type=f32)]
    pallas_call x4 -> x9, Pallas kernels: 27.9 us -> 39.3 us  [the longest x4 28 us: run_passes(): pl.pallas_call(functools.partial(passes_kernel, first, last, chunk, halo,...]
    all_to_all x2 -> x6, waiting for transfers between devices: 38.3 us -> 41.7 us  [exchange(): return lax.all_to_all(blocks, 'gy', split_axis=0, concat_axis=0, tiled=True)]
  transfers between devices with their start and end apart: 2 -> 6, of which waited for: 2 -> 6; matrix products, arithmetic and copies ran while one was open for 9% -> 1% of each run, Pallas kernels for 0% -> 13%
where the time goes in v2:
time: 191 us; the launch traced here: 188 us
  blocking collectives  46.2 us (24%)
  waiting for transfers between devices  41.7 us (22%)
  Pallas kernels  39.3 us (21%)
  starting transfers between devices  30.5 us (16%)
  local copies, waits for them, and re-layouts  30.2 us (16%)
    all_to_all x2, blocking collectives, exchange(): return lax.all_to_all(blocks, 'gy', split_axis=0, concat_axis=0, tiled=True)  46.2 us
    all_to_all x6, waiting for transfers between devices, exchange(): return lax.all_to_all(blocks, 'gy', split_axis=0, concat_axis=0, tiled=True)  41.7 us
    all_to_all x6, starting transfers between devices, exchange(): return lax.all_to_all(blocks, 'gy', split_axis=0, concat_axis=0, tiled=True)  30.5 us
    unnamed x68, local copies, waits for them, and re-layouts  28.9 us
    pallas_call x4, Pallas kernels, run_passes(): pl.pallas_call(functools.partial(passes_kernel, first, last, chunk, halo,...  28 us
    pallas_call x2, Pallas kernels, finish_filter(): pl.pallas_call(functools.partial(filter_kernel, first, not so_far, True,...  6.55 us
  transfers between devices with their start and end apart: 6, of which 6 were waited for; matrix products, arithmetic and copies ran while one was open for 1% of the time, Pallas kernels for 13%

profile of v2, /device:TPU:8, one launch (start us, length us, event | category | flops | bytes accessed | tf_op | source)
XLA Modules:
  0.0 188.1 jit_solution(15012573258700473552)
XLA Ops:
  0.0 1.3 fusion.1
  2.4 6.4 %all-to-all-start.1 = ((f32[16,1,32,256]{3,2,1,0:T(8,128)}), f32[16,1,32,256]{3,2,1,0:T(8,128)S(1)}, u32[]{:S(2)}, u32[]{:S(2)}) async-start(f32[16,1,32,256]{3,2,1,0:T(8,128)} %bitcast.18), calls=%async_computation.1 | async-start | bytes 1048576 | tf_op jit(solution)/shard_map/all_to_all | solution.py:456
  8.8 1.1 copy.22
  10.0 12.5 %all-to-all-done.1.refs_0_ = f32[16,1,32,256]{3,2,1,0:T(8,128)S(1)} async-done(((f32[16,1,32,256]{3,2,1,0:T(8,128)}), f32[16,1,32,256]{3,2,1,0:T(8,128)S(1)}, u32[]{:S(2)}, u32[]{:S(2)}) %all-to-all-start.1) | async-done | bytes 524320 | tf_op jit(solution)/shard_map/all_to_all | solution.py:456
  22.5 4.9 %all-to-all-start = ((f32[16,1,32,256]{3,2,1,0:T(8,128)}), f32[16,1,32,256]{3,2,1,0:T(8,128)S(1)}, u32[]{:S(2)}, u32[]{:S(2)}) async-start(f32[16,1,32,256]{3,2,1,0:T(8,128)} %bitcast.19), calls=%async_computation | async-start | bytes 1048576 | tf_op jit(solution)/shard_map/all_to_all | solution.py:456
  27.5 2.9 %shard_map.83 = (f32[1024,256]{1,0:T(8,128)S(1)}, f32[1024,256]{1,0:T(8,128)S(1)}, f32[1024,256]{1,0:T(8,128)S(1)}) custom-call(f32[16]{0:T(128)S(1)} %copy-done.18, bf16[256,640]{1,0:T(8,128)(2,1)S(1)} %pad.5.code_ref), custom_call_target="tpu_custom_call" | custom-call | flops 15728640 | bytes 3145728 | tf_op jit(solution)/shard_map/pallas_call | solution.py:106
  34.3 6.7 %all-to-all-done.refs_0_ = f32[16,1,32,256]{3,2,1,0:T(8,128)S(1)} async-done(((f32[16,1,32,256]{3,2,1,0:T(8,128)}), f32[16,1,32,256]{3,2,1,0:T(8,128)S(1)}, u32[]{:S(2)}, u32[]{:S(2)}) %all-to-all-start) | async-done | bytes 524320 | tf_op jit(solution)/shard_map/all_to_all | solution.py:456
  41.0 1.2 copy-done.22
  42.3 1.2 copy-done.24
  43.5 1.6 copy-done.25
  45.1 1.2 copy-done.27
  46.3 3.3 %shard_map.84 = (f32[16,1,48,256]{3,2,1,0:T(8,128)S(1)}, f32[16,1,32,256]{3,2,1,0:T(8,128)}, f32[1,1024,256]{2,1,0:T(8,128)S(1)}) custom-call(f32[16,1,32,256]{3,2,1,0:T(8,128)S(1)} %all-to-all-done.refs_0_, bf16[2,256,256]{2,1,0:T(8,128)(2,1)S(1)} %copy-done.3, bf16[2,2,512,256]{3,2,1,0:T(8,128)(2,1)S(1)} %copy-done.27, ...), custom_call_target="tpu_custom_call" | custom-call | flops 2415919104 | bytes 2097152 | tf_op jit(solution)/shard_map/pallas_call | solution.py:228
  49.6 24.3 %all_to_all.40 = f32[16,1,48,256]{3,2,1,0:T(8,128)S(1)} all-to-all(f32[16,1,48,256]{3,2,1,0:T(8,128)S(1)} %get-tuple-element.23), channel_id=1, replica_groups=mesh['groups'=2,'gy'=16] {'gy'}, dimensions={0} | all-to-all | bytes 1572864 | tf_op jit(solution)/shard_map/all_to_all | solution.py:456
  73.9 4.6 %all-to-all-start.3 = ((f32[16,1,32,256]{3,2,1,0:T(8,128)}), f32[16,1,32,256]{3,2,1,0:T(8,128)S(1)}, u32[]{:S(2)}, u32[]{:S(2)}) async-start(f32[16,1,32,256]{3,2,1,0:T(8,128)} %get-tuple-element.24), calls=%async_computation.3 | async-start | bytes 1048576 | tf_op jit(solution)/shard_map/all_to_all | solution.py:456
  78.5 6.8 %shard_map.86 = (f32[16,32,256]{2,1,0:T(8,128)S(1)}, f32[16,40,256]{2,1,0:T(8,128)S(1)}, f32[16,40,256]{2,1,0:T(8,128)S(1)}, f32[16,40,256]{2,1,0:T(8,128)S(1)}) custom-call(s32[1]{0:T(128)} %bitcast.start_ref, f32[16,48,256]{2,1,0:T(8,128)S(1)} %bitcast.20), custom_call_target="tpu_custom_call" | custom-call | flops 23592960 | bytes 6291456 | tf_op jit(solution)/shard_map/pallas_call | solution.py:433
  88.6 3.5 %all-to-all-done.3 = f32[16,1,32,256]{3,2,1,0:T(8,128)S(1)} async-done(((f32[16,1,32,256]{3,2,1,0:T(8,128)}), f32[16,1,32,256]{3,2,1,0:T(8,128)S(1)}, u32[]{:S(2)}, u32[]{:S(2)}) %all-to-all-start.3) | async-done | bytes 524320 | tf_op jit(solution)/shard_map/all_to_all | solution.py:456
  92.1 4.9 %all-to-all-start.5 = ((f32[16,1,32,256]{3,2,1,0:T(8,128)}), f32[16,1,32,256]{3,2,1,0:T(8,128)S(1)}, u32[]{:S(2)}, u32[]{:S(2)}) async-start(f32[16,1,32,256]{3,2,1,0:T(8,128)} %bitcast.26), calls=%async_computation.5 | async-start | bytes 1048576 | tf_op jit(solution)/shard_map/all_to_all | solution.py:456
  97.1 6.8 %shard_map.85 = (f32[16,32,256]{2,1,0:T(8,128)S(1)}, f32[16,40,256]{2,1,0:T(8,128)S(1)}, f32[16,40,256]{2,1,0:T(8,128)S(1)}, f32[16,40,256]{2,1,0:T(8,128)S(1)}) custom-call(s32[1]{0:T(128)} %bitcast.start_ref, f32[16,48,256]{2,1,0:T(8,128)S(1)} %bitcast.21, f32[16,32,256]{2,1,0:T(8,128)S(1)} %bitcast.24), custom_call_target="tpu_custom_call" | custom-call | flops 23592960 | bytes 6291456 | tf_op jit(solution)/shard_map/pallas_call | solution.py:433
  107.2 3.5 %all-to-all-done.5.refs_0_ = f32[16,1,32,256]{3,2,1,0:T(8,128)S(1)} async-done(((f32[16,1,32,256]{3,2,1,0:T(8,128)}), f32[16,1,32,256]{3,2,1,0:T(8,128)S(1)}, u32[]{:S(2)}, u32[]{:S(2)}) %all-to-all-start.5) | async-done | bytes 524320 | tf_op jit(solution)/shard_map/all_to_all | solution.py:456
  110.7 4.9 %all-to-all-start.4 = ((f32[16,1,32,256]{3,2,1,0:T(8,128)}), f32[16,1,32,256]{3,2,1,0:T(8,128)S(1)}, u32[]{:S(2)}, u32[]{:S(2)}) async-start(f32[16,1,32,256]{3,2,1,0:T(8,128)} %bitcast.27), calls=%async_computation.4 | async-start | bytes 1048576 | tf_op jit(solution)/shard_map/all_to_all | solution.py:456
  117.5 11.7 %all-to-all-done.4.refs_0_ = f32[16,1,32,256]{3,2,1,0:T(8,128)S(1)} async-done(((f32[16,1,32,256]{3,2,1,0:T(8,128)}), f32[16,1,32,256]{3,2,1,0:T(8,128)S(1)}, u32[]{:S(2)}, u32[]{:S(2)}) %all-to-all-start.4) | async-done | bytes 524320 | tf_op jit(solution)/shard_map/all_to_all | solution.py:456
  129.3 1.2 copy-done.2
  130.5 1.2 copy-done.20
  131.7 1.6 copy-done.26
  133.3 1.2 copy-done.28
  134.5 1.2 copy-done.30
  135.8 3.3 %shard_map.88 = (f32[16,1,40,256]{3,2,1,0:T(8,128)S(1)}, f32[16,1,32,256]{3,2,1,0:T(8,128)}) custom-call(f32[16,1,32,256]{3,2,1,0:T(8,128)S(1)} %all-to-all-done.4.refs_0_, bf16[2,256,256]{2,1,0:T(8,128)(2,1)S(1)} %copy-done.3, bf16[2,2,512,256]{3,2,1,0:T(8,128)(2,1)S(1)} %copy-done.28, f32[1,1024,256]{2,1,0:T(8,128)S(1)} %copy-done.2, ...), custom_call_target="tpu_custom_call" | custom-call | flops 2415919104 | bytes 2097152 | tf_op jit(solution)/shard_map/pallas_call | solution.py:228
  139.1 21.9 %all_to_all.41 = f32[16,1,40,256]{3,2,1,0:T(8,128)S(1)} all-to-all(f32[16,1,40,256]{3,2,1,0:T(8,128)S(1)} %get-tuple-element.29), channel_id=1, replica_groups=mesh['groups'=2,'gy'=16] {'gy'}, dimensions={0} | all-to-all | bytes 1310720 | tf_op jit(solution)/shard_map/all_to_all | solution.py:456
  161.0 4.7 %all-to-all-start.7 = ((f32[16,1,32,256]{3,2,1,0:T(8,128)}), f32[16,1,32,256]{3,2,1,0:T(8,128)S(1)}, u32[]{:S(2)}, u32[]{:S(2)}) async-start(f32[16,1,32,256]{3,2,1,0:T(8,128)} %get-tuple-element.30), calls=%async_computation.7 | async-start | bytes 1048576 | tf_op jit(solution)/shard_map/all_to_all | solution.py:456
  168.9 6.7 %shard_map.89.refs_5_ = f32[512,256]{1,0:T(8,128)S(1)} custom-call(s32[1]{0:T(128)} %bitcast.start_ref, f32[16,40,256]{2,1,0:T(8,128)S(1)} %bitcast.22, f32[16,40,256]{2,1,0:T(8,128)S(1)} %copy-done.11, f32[16,40,256]{2,1,0:T(8,128)S(1)} %copy-done.13, f32[16,40,256]{2,1,0:T(8,128)S(1)} %copy-done.15), custom_call_target="tpu_custom_call" | custom-call | flops 19660800 | bytes 5242880 | tf_op jit(solution)/shard_map/pallas_call | solution.py:433
  175.6 3.7 %all-to-all-done.7 = f32[16,1,32,256]{3,2,1,0:T(8,128)S(1)} async-done(((f32[16,1,32,256]{3,2,1,0:T(8,128)}), f32[16,1,32,256]{3,2,1,0:T(8,128)S(1)}, u32[]{:S(2)}, u32[]{:S(2)}) %all-to-all-start.7) | async-done | bytes 524320 | tf_op jit(solution)/shard_map/all_to_all | solution.py:456
  180.4 7.7 %shard_map.90 = f32[1024,256]{1,0:T(8,128)} custom-call(s32[1]{0:T(128)} %bitcast.start_ref, f32[16,40,256]{2,1,0:T(8,128)S(1)} %bitcast.23, f32[16,32,256]{2,1,0:T(8,128)S(1)} %bitcast.25, f32[16,40,256]{2,1,0:T(8,128)S(1)} %copy-done.5, f32[16,40,256]{2,1,0:T(8,128)S(1)} %copy-done.7, f32[16,40,256]{2,1,0:T(8,128)S(1)} %copy-done.9, ...), custom_call_target="tpu_custom_call" | custom-call | flops 19660800 | bytes 5242880 | tf_op jit(solution)/shard_map/pallas_call | solution.py:433
  (62 shorter events, 18.0 us)
Async XLA Ops:
  1.3 26.1 %copy-start.31 = (s32[513,129]{0,1:T(8,128)S(1)}, s32[513,129]{0,1:T(8,128)}, u32[]{:S(2)}) copy-start(s32[513,129]{0,1:T(8,128)} %param.10) | copy-start | bytes 794128
  1.3 26.1 %copy-start.32 = (s32[513,129]{0,1:T(8,128)S(1)}, s32[513,129]{0,1:T(8,128)}, u32[]{:S(2)}) copy-start(s32[513,129]{0,1:T(8,128)} %param.11) | copy-start | bytes 794128
  2.4 25.1 %copy-start.18 = (f32[16]{0:T(128)S(1)}, f32[16]{0:T(128)}, u32[]{:S(2)}) copy-start(f32[16]{0:T(128)} %table_ref.1) | copy-start | bytes 196
  2.4 20.1 %all-to-all-start.1 = ((f32[16,1,32,256]{3,2,1,0:T(8,128)}), f32[16,1,32,256]{3,2,1,0:T(8,128)S(1)}, u32[]{:S(2)}, u32[]{:S(2)}) async-start(f32[16,1,32,256]{3,2,1,0:T(8,128)} %bitcast.18), calls=%async_computation.1 | async-start | bytes 1048576 | tf_op jit(solution)/shard_map/all_to_all | solution.py:456
  8.8 24.6 %copy-start = (bf16[2,2,512,256]{3,2,1,0:T(8,128)(2,1)S(1)}, bf16[2,2,512,256]{3,2,1,0:T(8,128)(2,1)}, u32[]{:S(2)}) copy-start(bf16[2,2,512,256]{3,2,1,0:T(8,128)(2,1)} %constant.22.clone.refs_2_) | copy-start | bytes 3145732
  8.8 24.6 %copy-start.3 = (bf16[2,256,256]{2,1,0:T(8,128)(2,1)S(1)}, bf16[2,256,256]{2,1,0:T(8,128)(2,1)}, u32[]{:S(2)}) copy-start(bf16[2,256,256]{2,1,0:T(8,128)(2,1)} %constant.21.clone.refs_1_) | copy-start | bytes 786436
  22.5 18.6 %all-to-all-start = ((f32[16,1,32,256]{3,2,1,0:T(8,128)}), f32[16,1,32,256]{3,2,1,0:T(8,128)S(1)}, u32[]{:S(2)}, u32[]{:S(2)}) async-start(f32[16,1,32,256]{3,2,1,0:T(8,128)} %bitcast.19), calls=%async_computation | async-start | bytes 1048576 | tf_op jit(solution)/shard_map/all_to_all | solution.py:456
  30.5 1.0 copy-start.19
  31.4 1.0 copy-start.21
  32.4 1.0 copy-start.23
  41.0 1.2 copy-start.22
  42.3 1.2 copy-start.24
  43.5 1.6 copy-start.25
  45.1 1.2 copy-start.27
  49.6 24.3 %copy-start.29 = (f32[1,1024,256]{2,1,0:T(8,128)}, f32[1,1024,256]{2,1,0:T(8,128)S(1)}, u32[]{:S(2)}) copy-start(f32[1,1024,256]{2,1,0:T(8,128)S(1)} %get-tuple-element.27.refs_5_) | copy-start | bytes 3145732
  73.9 18.2 %all-to-all-start.3 = ((f32[16,1,32,256]{3,2,1,0:T(8,128)}), f32[16,1,32,256]{3,2,1,0:T(8,128)S(1)}, u32[]{:S(2)}, u32[]{:S(2)}) async-start(f32[16,1,32,256]{3,2,1,0:T(8,128)} %get-tuple-element.24), calls=%async_computation.3 | async-start | bytes 1048576 | tf_op jit(solution)/shard_map/all_to_all | solution.py:456
  92.1 18.6 %all-to-all-start.5 = ((f32[16,1,32,256]{3,2,1,0:T(8,128)}), f32[16,1,32,256]{3,2,1,0:T(8,128)S(1)}, u32[]{:S(2)}, u32[]{:S(2)}) async-start(f32[16,1,32,256]{3,2,1,0:T(8,128)} %bitcast.26), calls=%async_computation.5 | async-start | bytes 1048576 | tf_op jit(solution)/shard_map/all_to_all | solution.py:456
  104.7 0.9 copy-start.6
  110.7 18.6 %all-to-all-start.4 = ((f32[16,1,32,256]{3,2,1,0:T(8,128)}), f32[16,1,32,256]{3,2,1,0:T(8,128)S(1)}, u32[]{:S(2)}, u32[]{:S(2)}) async-start(f32[16,1,32,256]{3,2,1,0:T(8,128)} %bitcast.27), calls=%async_computation.4 | async-start | bytes 1048576 | tf_op jit(solution)/shard_map/all_to_all | solution.py:456
  116.6 1.0 copy-start.1
  129.3 1.2 copy-start.2
  130.5 1.2 copy-start.20
  131.7 1.6 copy-start.26
  133.3 1.2 copy-start.28
  134.5 1.2 copy-start.30
  161.0 18.3 %copy-start.5 = (f32[16,40,256]{2,1,0:T(8,128)S(1)}, f32[16,40,256]{2,1,0:T(8,128)}, u32[]{:S(2)}) copy-start(f32[16,40,256]{2,1,0:T(8,128)} %copy-done.4) | copy-start | bytes 1966084
  161.0 18.3 %copy-start.7 = (f32[16,40,256]{2,1,0:T(8,128)S(1)}, f32[16,40,256]{2,1,0:T(8,128)}, u32[]{:S(2)}) copy-start(f32[16,40,256]{2,1,0:T(8,128)} %copy-done.6) | copy-start | bytes 1966084
  161.0 18.3 %all-to-all-start.7 = ((f32[16,1,32,256]{3,2,1,0:T(8,128)}), f32[16,1,32,256]{3,2,1,0:T(8,128)S(1)}, u32[]{:S(2)}, u32[]{:S(2)}) async-start(f32[16,1,32,256]{3,2,1,0:T(8,128)} %get-tuple-element.30), calls=%async_computation.7 | async-start | bytes 1048576 | tf_op jit(solution)/shard_map/all_to_all | solution.py:456
  165.6 1.1 copy-start.11
  166.7 1.1 copy-start.13
  167.8 1.1 copy-start.15
  179.3 1.1 copy-start.9
  (7 other events, 5.8 us)

commit v3 on v1

v3 whole, which is shorter than its diff:
```python
import functools

import jax
import jax.numpy as jnp
import ml_dtypes
import numpy as np
from jax import lax
from jax.experimental import pallas as pl
from jax.experimental.pallas import tpu as pltpu
from jax.sharding import PartitionSpec as P

OUTER = 2
PASSES = 2

step_dual = 0.14
step_primal = 0.14
huber_eps = 0.05
bound_dual = 0.5

SUB = 8
LANE = 128
HALO_LAST = 2 * PASSES
HALO_FIRST = HALO_LAST + 2 * PASSES - 2
UNROLL = 4
MIB = 1024 * 1024

f32 = jnp.float32
bf16 = jnp.bfloat16


def halves(table):
    high = table.astype(ml_dtypes.bfloat16)
    low = (table - high.astype(np.float64)).astype(ml_dtypes.bfloat16)
    return np.stack([high, low])


def cas(rows, columns, length):
    phase = (rows[:, None] * columns[None, :]) % length
    angle = phase * (2.0 * np.pi / length)
    return np.cos(angle) + np.sin(angle)


def z_table(length):
    index = np.arange(length)
    return halves(cas(index, index, length))


def x_tables(length):
    half = length // 2
    place = np.arange(half)
    even = cas(2 * place, place, length)
    odd = cas(2 * place + 1, place, length)
    return np.stack([halves(even), halves(odd), halves(odd.T)])


def padded_to(length, unit):
    return -(-length // unit) * unit


def weights_kernel(nx, nz, levels, table_ref, code_ref, both, data, prior):
    half = nx // 2
    tile = min(256, half)
    heights, widths = code_ref.shape
    scale = 1.0 / (nx * nz)
    kz = lax.broadcasted_iota(jnp.int32, (heights, nz), 1)
    kz = jnp.minimum(kz, nz - kz)
    pick_z = jnp.where(kz == lax.broadcasted_iota(jnp.int32, (heights, nz), 0), 1.0, 0.0)
    pick_z = pick_z.astype(bf16)
    for part in range(2):
        for top in range(0, half, tile):
            kx = 2 * (top + lax.broadcasted_iota(jnp.int32, (tile, widths), 0)) + part
            kx = jnp.minimum(kx, nx - kx)
            pick_x = jnp.where(kx == lax.broadcasted_iota(jnp.int32, (tile, widths), 1), 1.0, 0.0)
            tall = lax.dot_general(
                pick_x.astype(bf16),
                code_ref[...],
                (((1,), (1,)), ((), ())),
                preferred_element_type=f32,
            )
            spread = jnp.dot(tall.astype(bf16), pick_z, preferred_element_type=f32)
            response = jnp.zeros_like(spread)
            for level in range(levels):
                response = jnp.where(spread == level + 1.0, table_ref[level], response)
            gain = scale / (response * response + 1.0)
            rows = slice(part * half + top, part * half + top + tile)
            prior[rows] = gain
            data[rows] = response * gain
            both[rows] = response * gain + gain


def make_weights(tf_table, tilt_index, wedge, nx, nz):
    levels = tf_table.shape[0]
    code = jnp.where(wedge > 0, tilt_index + 1, 0).T
    extra = [(0, padded_to(size, LANE) - size) for size in code.shape]
    code = jnp.pad(code, extra).astype(bf16)
    grid = jax.ShapeDtypeStruct((nx, nz), f32)
    vmem = pl.BlockSpec(memory_space=pltpu.VMEM)
    return pl.pallas_call(
        functools.partial(weights_kernel, nx, nz, levels),
        in_specs=[pl.BlockSpec(memory_space=pltpu.SMEM), vmem],
        out_specs=[vmem] * 3,
        out_shape=[grid] * 3,
        compiler_params=pltpu.CompilerParams(vmem_limit_bytes=16 * MIB),
        cost_estimate=pl.CostEstimate(
            flops=60 * nx * nz, bytes_accessed=12 * nx * nz, transcendentals=0
        ),
    )(tf_table, code)


def split(value):
    high = value.astype(bf16)
    return high, (value - high.astype(f32)).astype(bf16)


def dot3(a, b):
    dot = functools.partial(jnp.dot, preferred_element_type=f32)
    return dot(a[0], b[0]) + (dot(a[0], b[1]) + dot(a[1], b[0]))


def turn_kernel(ny, planes, cells, turned, staged, placed, semaphores):
    blocks = len(staged)
    steps = placed.shape[1] // planes
    rows = planes * ny
    incoming = [
        [
            pltpu.make_async_copy(
                cells.at[pl.ds(step * rows, rows), pl.ds(LANE * k, LANE)],
                staged[k].at[pl.ds(step * rows, rows), :],
                semaphores.at[0, step, k],
            )
            for k in range(blocks)
        ]
        for step in range(steps)
    ]
    outgoing = [
        pltpu.make_async_copy(
            placed.at[:, pl.ds(step * planes, planes), :],
            turned.at[:, pl.ds(step * planes, planes), :],
            semaphores.at[1, step, 0],
        )
        for step in range(steps)
    ]
    for step in range(steps):
        for copy in incoming[step]:
            copy.start()
    for step in range(steps):
        for copy in incoming[step]:
            copy.wait()
        for y in range(ny):
            for x in range(step * planes, (step + 1) * planes, SUB):
                for k in range(blocks):
                    placed[y, x : x + SUB, LANE * k : LANE * (k + 1)] = staged[k][
                        pl.ds(x * ny + y, SUB, stride=ny), :
                    ]
        outgoing[step].start()
    for copy in outgoing:
        copy.wait()


def turn(observed):
    slab, ny, nz = observed.shape
    planes = 2 * SUB if slab % (2 * SUB) == 0 else SUB
    anywhere = pl.BlockSpec(memory_space=pl.ANY)
    return pl.pallas_call(
        functools.partial(turn_kernel, ny, planes),
        in_specs=[anywhere],
        out_specs=anywhere,
        out_shape=jax.ShapeDtypeStruct((ny, slab, nz), f32),
        scratch_shapes=[
            [pltpu.VMEM((slab * ny, LANE), f32)] * (nz // LANE),
            pltpu.VMEM((ny, slab, nz), f32),
            pltpu.SemaphoreType.DMA((2, slab // planes, nz // LANE)),
        ],
        compiler_params=pltpu.CompilerParams(vmem_limit_bytes=16 * MIB),
        cost_estimate=pl.CostEstimate(
            flops=0, bytes_accessed=8 * slab * ny * nz, transcendentals=0
        ),
    )(observed.reshape(slab * ny, nz))


def window_tiles(width, nz):
    return width * nz // (SUB * LANE)


def filter_kernel(first, halo, slab, *refs):
    cells, ztab, xtab_far, refs = refs[0], refs[1], refs[2], refs[3:]
    if first:
        both_far, data_far, windows, kept_far, refs = refs[0], refs[1], refs[2], refs[3], refs[4:]
    else:
        kept_far, prior_far, windows, refs = refs[0], refs[1], refs[2], refs[3:]
    xtab, scale, other, high, low, padded, semaphores = refs
    devices, rows, _, nz = cells.shape
    nx = devices * slab
    half = nx // 2
    tile = min(256, half)
    width = slab + 2 * halo
    blocks = nz // LANE
    ztable = (ztab[0], ztab[1])
    arrivals = [
        pltpu.make_async_copy(xtab_far.at[0], xtab.at[0], semaphores.at[0]),
        pltpu.make_async_copy(xtab_far.at[1], xtab.at[1], semaphores.at[1]),
        pltpu.make_async_copy(both_far if first else prior_far, scale, semaphores.at[2]),
        pltpu.make_async_copy(xtab_far.at[2], xtab.at[2], semaphores.at[3]),
    ]
    if first:
        arrivals.append(pltpu.make_async_copy(data_far, other.at[0], semaphores.at[4]))
    for copy in arrivals:
        copy.start()
    for r in range(rows):
        if not first:
            kept_copy = pltpu.make_async_copy(kept_far.at[r], other.at[0], semaphores.at[4])
            kept_copy.start()
        flat = cells[:, r].reshape(nx, nz)
        for top in range(0, half, tile):
            a = dot3(split(flat[top : top + tile]), ztable)
            b = dot3(split(flat[half + top : half + top + tile]), ztable)
            for spot, value in ((top, a + b), (half + top, a - b)):
                high[spot : spot + tile], low[spot : spot + tile] = split(value)
        folded = [
            (high[part * half : (part + 1) * half], low[part * half : (part + 1) * half])
            for part in range(2)
        ]
        waves = []
        for part in range(2):
            if r == 0:
                arrivals[part].wait()
            for top in range(0, half, tile):
                table = (xtab[part, 0, top : top + tile], xtab[part, 1, top : top + tile])
                waves.append(dot3(table, folded[part]))
        if r == 0:
            arrivals[2].wait()
            if first:
                arrivals[4].wait()
        if not first:
            kept_copy.wait()
        for i, wave in enumerate(waves):
            spot = slice(i * tile, (i + 1) * tile)
            if first:
                mixed = wave * scale[spot]
                other[1, spot] = wave * other[0, spot]
            else:
                mixed = other[0, spot] + wave * scale[spot]
            high[spot], low[spot] = split(mixed)
        if first:
            kept_copy = pltpu.make_async_copy(other.at[1], kept_far.at[r], semaphores.at[5])
            kept_copy.start()
        if r == 0:
            arrivals[3].wait()
        even = (high[:half], low[:half])
        odd = (high[half:], low[half:])
        after = (halo + nx) // SUB * SUB
        padded[:SUB] = jnp.zeros((SUB, nz), f32)
        padded[after : after + 2 * SUB] = jnp.zeros((2 * SUB, nz), f32)
        for top in range(0, half, tile):
            e = dot3((xtab[0, 0, top : top + tile], xtab[0, 1, top : top + tile]), even)
            o = dot3((xtab[2, 0, top : top + tile], xtab[2, 1, top : top + tile]), odd)
            padded[halo + top : halo + top + tile] = dot3(split(e + o), ztable)
            padded[halo + half + top : halo + half + top + tile] = dot3(split(e - o), ztable)
        for device in range(devices):
            for g in range(width // SUB):
                spot = device * slab + SUB * g
                for k in range(blocks):
                    windows[device, r, g * blocks + k] = padded[
                        spot : spot + SUB, LANE * k : LANE * (k + 1)
                    ]
            spot = device * slab + width // SUB * SUB
            rest = width % SUB
            for k in range(blocks if rest else 0):
                windows[
                    device, r, width // SUB * blocks + k * rest // SUB, k * rest % SUB : k * rest % SUB + rest
                ] = padded[spot : spot + rest, LANE * k : LANE * (k + 1)]
        if first:
            kept_copy.wait()


def run_filter(first, halo, cells, tables, far):
    devices, rows, slab, nz = cells.shape
    nx = devices * slab
    ztab, xtab = tables
    vmem = pl.BlockSpec(memory_space=pltpu.VMEM)
    anywhere = pl.BlockSpec(memory_space=pl.ANY)
    tiles = window_tiles(slab + 2 * halo, nz)
    out_shape = [jax.ShapeDtypeStruct((devices, rows, tiles, SUB, LANE), f32)]
    out_specs = [vmem]
    if first:
        out_shape.append(jax.ShapeDtypeStruct((rows, nx, nz), f32))
        out_specs.append(anywhere)
    return pl.pallas_call(
        functools.partial(filter_kernel, first, halo, slab),
        in_specs=[vmem, vmem, anywhere, anywhere, anywhere],
        out_specs=out_specs,
        out_shape=out_shape,
        scratch_shapes=[
            pltpu.VMEM(xtab.shape, bf16),
            pltpu.VMEM((nx, nz), f32),
            pltpu.VMEM((2, nx, nz), f32),
            pltpu.VMEM((nx, nz), bf16),
            pltpu.VMEM((nx, nz), bf16),
            pltpu.VMEM((nx + 3 * SUB, nz), f32),
            pltpu.SemaphoreType.DMA((6,)),
        ],
        compiler_params=pltpu.CompilerParams(vmem_limit_bytes=32 * MIB),
        cost_estimate=pl.CostEstimate(
            flops=6 * rows * nx * nz * (2 * nz + nx),
            bytes_accessed=8 * rows * nx * nz,
            transcendentals=0,
        ),
    )(cells, ztab, xtab, *far)


def lane_sums(pieces):
    lane = lax.broadcasted_iota(jnp.int32, pieces[0].shape, 1)
    up = [pltpu.roll(piece, LANE - 1, 1) for piece in pieces]
    down = [pltpu.roll(piece, 1, 1) for piece in pieces]
    sums = []
    for k in range(len(pieces)):
        above = up[k + 1] if k + 1 < len(pieces) else 0.0
        below = down[k - 1] if k > 0 else 0.0
        sums.append(
            jnp.where(lane == LANE - 1, above, up[k]) + jnp.where(lane == 0, below, down[k])
        )
    return sums


def row_sums(groups):
    row = lax.broadcasted_iota(jnp.int32, groups[0].shape, 0)
    up = [pltpu.roll(group, SUB - 1, 0) for group in groups]
    down = [pltpu.roll(group, 1, 0) for group in groups]
    count = len(groups)
    return [
        jnp.where(row == SUB - 1, up[(g + 1) % count], up[g])
        + jnp.where(row == 0, down[g - 1], down[g])
        for g in range(count)
    ]


def passes_kernel(first, last, halo, slab, nx, start_ref, target, *refs):
    if first:
        duals_in, refs = None, refs
    else:
        duals_in, refs = refs[:3], refs[3:]
    if last:
        restored, refs = refs[0], refs[1:]
    else:
        current, duals_out, refs = refs[0], refs[1:4], refs[4:]
    lead, field, dual_x, dual_y, dual_z = refs[:5]
    turned = refs[5:]
    ny, _, nz = field.shape
    width = slab + 2 * halo
    groups = padded_to(width, SUB) // SUB
    blocks = nz // LANE
    decay = 1.0 / (1.0 + step_dual * huber_eps / bound_dual)
    gain = step_dual * decay
    floor = 1.0 / (decay * decay)
    slope = (gain / (decay * bound_dual)) ** 2
    keep = 1.0 / (1.0 + step_primal)
    pull = step_primal * keep
    push = pull * gain / decay
    origin = start_ref[0] - halo

    def goal_of(y, g, k):
        if SUB * (g + 1) <= width:
            return target[y, g * blocks + k]
        rest = width % SUB
        tail = target[y, g * blocks + k * rest // SUB]
        shift = k * rest % SUB
        return pltpu.roll(tail, SUB - shift, 0) if shift else tail

    def masked(value, g):
        if SUB * g >= halo and SUB * (g + 1) <= width - halo:
            return value
        place = origin + SUB * g + lax.broadcasted_iota(jnp.int32, (SUB, LANE), 0)
        return jnp.where((place >= 0) & (place < nx), value, 0.0)

    def at(g, k):
        return pl.ds(SUB * g, SUB), pl.ds(LANE * k, LANE)

    empty = jnp.zeros(lead.shape[1:], f32)
    for plane in (0, ny + 1):
        lead[plane] = empty
        dual_y[plane] = empty

    @pl.loop(0, ny, unroll=UNROLL)
    def _(y):
        for g in range(groups):
            for k in range(blocks):
                lead[(y + 1,) + at(g, k)] = goal_of(y, g, k)

    for sweep in range(PASSES):
        final = sweep == PASSES - 1

        @pl.loop(0, ny, unroll=UNROLL)
        def _(y):
            here = [[lead[(y + 1,) + at(g, k)] for k in range(blocks)] for g in range(groups)]
            columns = [row_sums([here[g][k] for g in range(groups)]) for k in range(blocks)]
            for g in range(groups):
                along_z = lane_sums(here[g])
                for k in range(blocks):
                    spot = at(g, k)
                    twice = here[g][k] + here[g][k]
                    along_y = lead[(y,) + spot] + lead[(y + 2,) + spot]
                    raised = [columns[k][g] - twice, along_y - twice, along_z[k] - twice]
                    if sweep > 0:
                        before = [dual_x[(y,) + spot], dual_y[(y + 1,) + spot], dual_z[(y,) + spot]]
                    elif duals_in is not None:
                        before = [ref[(y,) + spot] for ref in duals_in]
                    else:
                        before = None
                    if before is not None:
                        raised = [old + new for old, new in zip(before, raised)]
                    total = (
                        raised[0] * raised[0] + raised[1] * raised[1] + raised[2] * raised[2]
                    )
                    shrink = lax.rsqrt(jnp.maximum(floor, total * slope))
                    made = [raised[0] * masked(shrink, g), raised[1] * shrink, raised[2] * shrink]
                    dual_x[(y,) + spot] = made[0]
                    dual_y[(y + 1,) + spot] = made[1]
                    dual_z[(y,) + spot] = made[2]
                    if final and not last:
                        shift = halo - HALO_LAST
                        lo = max(0, shift - SUB * g)
                        hi = min(SUB, slab + 2 * HALO_LAST + shift - SUB * g)
                        if lo < hi:
                            rows = pl.ds(SUB * g + lo - shift, hi - lo)
                            for a in range(3):
                                duals_out[a][y, rows, spot[1]] = made[a][lo:hi]

        @pl.loop(0, ny, unroll=UNROLL)
        def _(y):
            wanted = range(groups)
            if final:
                wanted = [
                    g for g in wanted if SUB * (g + 1) > halo and SUB * g < width - halo
                ]
            near = [[dual_x[(y,) + at(g, k)] for k in range(blocks)] for g in range(groups)]
            columns = [row_sums([near[g][k] for g in range(groups)]) for k in range(blocks)]
            for g in wanted:
                here = [dual_z[(y,) + at(g, k)] for k in range(blocks)]
                along_z = lane_sums(here)
                for k in range(blocks):
                    spot = at(g, k)
                    along_y = dual_y[(y,) + spot] + dual_y[(y + 2,) + spot]
                    centre = near[g][k] + dual_y[(y + 1,) + spot] + here[k]
                    adjoint = columns[k][g] + along_y + along_z[k] - (centre + centre)
                    move = push * adjoint
                    goal = goal_of(y, g, k)
                    if sweep == 0:
                        updated = goal - move
                        ahead = updated - move
                    else:
                        old = field[(y,) + spot]
                        updated = keep * old + pull * goal - move
                        ahead = updated + updated - old
                    if not final:
                        field[(y,) + spot] = updated
                        lead[(y + 1,) + spot] = masked(ahead, g)
                        continue
                    lo = max(0, halo - SUB * g)
                    hi = min(SUB, slab + halo - SUB * g)
                    x = SUB * g + lo - halo
                    if last:
                        turned[k][pl.ds(x * ny + y, hi - lo, stride=ny), :] = updated[lo:hi]
                    else:
                        current[y, pl.ds(x, hi - lo), spot[1]] = updated[lo:hi]

    for k, block in enumerate(turned):
        restored[:, LANE * k : LANE * (k + 1)] = block[:]


def run_passes(first, last, halo, slab, nx, start, target, duals):
    ny = target.shape[0]
    nz = target.shape[1] * SUB * LANE // (slab + 2 * halo)
    width = padded_to(slab + 2 * halo, SUB)
    vmem = pl.BlockSpec(memory_space=pltpu.VMEM)
    if last:
        out_shape = jax.ShapeDtypeStruct((slab * ny, nz), f32)
        out_specs = vmem
    else:
        kept = jax.ShapeDtypeStruct((ny, slab + 2 * HALO_LAST, nz), f32)
        out_shape = [jax.ShapeDtypeStruct((ny, slab, nz), f32), kept, kept, kept]
        out_specs = [vmem] * 4
    return pl.pallas_call(
        functools.partial(passes_kernel, first, last, halo, slab, nx),
        in_specs=[pl.BlockSpec(memory_space=pltpu.SMEM)] + [vmem] * (1 + len(duals)),
        out_specs=out_specs,
        out_shape=out_shape,
        scratch_shapes=[
            pltpu.VMEM((ny + 2, width, nz), f32),
            pltpu.VMEM((ny, width, nz), f32),
            pltpu.VMEM((ny, width, nz), f32),
            pltpu.VMEM((ny + 2, width, nz), f32),
            pltpu.VMEM((ny, width, nz), f32),
        ]
        + [pltpu.VMEM((slab * ny, LANE), f32)] * (nz // LANE if last else 0),
        compiler_params=pltpu.CompilerParams(vmem_limit_bytes=40 * MIB),
        cost_estimate=pl.CostEstimate(
            flops=60 * PASSES * ny * width * nz,
            bytes_accessed=8 * 4 * ny * width * nz,
            transcendentals=PASSES * ny * width * nz,
        ),
    )(start, target, *duals)


def exchange(blocks):
    return lax.all_to_all(blocks, "gy", split_axis=0, concat_axis=0, tiled=True)


def local(observed, tf_table, tilt_index, wedge):
    slab, ny, nz = observed.shape
    devices = lax.axis_size("gy")
    rows = ny // devices
    nx = slab * devices
    start = (lax.axis_index("gy") * slab).astype(jnp.int32).reshape(1)
    tables = (jnp.asarray(z_table(nz)), jnp.asarray(x_tables(nx)))
    cells = exchange(turn(observed).reshape(devices, rows, slab, nz))
    both, data, prior = make_weights(tf_table, tilt_index, wedge, nx, nz)
    duals = ()
    for outer in range(OUTER):
        first, last = outer == 0, outer == OUTER - 1
        halo = HALO_LAST if last else HALO_FIRST
        made = run_filter(first, halo, cells, tables, (both, data) if first else (kept, prior))
        if first:
            kept = made[1]
        windows = exchange(made[0])
        target = windows.reshape((ny,) + windows.shape[2:])
        made = run_passes(first, last, halo, slab, nx, start, target, duals)
        if last:
            return made.reshape(slab, ny, nz)
        duals = tuple(made[1:])
        cells = exchange(made[0].reshape(devices, rows, slab, nz))


def solution(mesh):
    in_specs = (P(("groups", "gy"), None, None), P(), P(), P())
    out_specs = P(("groups", "gy"), None, None)
    return jax.shard_map(local, mesh=mesh, in_specs=in_specs, out_specs=out_specs, check_vma=False)
```

time: 167 us -> 159 us (0.952)
  matrix products: 14.7 us -> 0 us
  waiting for transfers between devices: 38.3 us -> 47.9 us
  Pallas kernels: 27.9 us -> 23.9 us
  local copies, waits for them, and re-layouts: 6.97 us -> 9.04 us
    dot_general x1 -> x0, matrix products: 14.7 us -> none  [filters(): spread = jnp.dot(pick_x, wide, preferred_element_type=f32)]
    all_to_all x2, waiting for transfers between devices: 38.3 us -> 47.9 us  [exchange(): return lax.all_to_all(blocks, 'gy', split_axis=0, concat_axis=0, tiled=True)]
    pallas_call x2, Pallas kernels: 17.1 us -> 10.4 us  [run_passes(): pl.pallas_call(functools.partial(passes_kernel, first, last, halo, slab,...]
    unnamed x19 -> x24, local copies, waits for them, and re-layouts: 6.25 us -> 9.02 us
    pallas_call x2 -> x4, Pallas kernels: 10.8 us -> 13.4 us  [the longest x2 9.23 us: run_filter(): pl.pallas_call(functools.partial(filter_kernel, first, halo, slab), in_sp...]
  transfers between devices with their start and end apart: 2 -> 2, of which waited for: 2 -> 2; matrix products, arithmetic and copies ran while one was open for 9% -> 0% of each run, Pallas kernels for 0% -> 2%
where the time goes in v3:
time: 159 us; the launch traced here: 157 us
  blocking collectives  63.7 us (40%)
  waiting for transfers between devices  47.9 us (30%)
  Pallas kernels  23.9 us (15%)
  starting transfers between devices  12.2 us (8%)
  local copies, waits for them, and re-layouts  9.04 us (6%)
    all_to_all x2, blocking collectives, exchange(): return lax.all_to_all(blocks, 'gy', split_axis=0, concat_axis=0, tiled=True)  63.7 us
    all_to_all x2, waiting for transfers between devices, exchange(): return lax.all_to_all(blocks, 'gy', split_axis=0, concat_axis=0, tiled=True)  47.9 us
    all_to_all x2, starting transfers between devices, exchange(): return lax.all_to_all(blocks, 'gy', split_axis=0, concat_axis=0, tiled=True)  12.2 us
    pallas_call x2, Pallas kernels, run_passes(): pl.pallas_call(functools.partial(passes_kernel, first, last, halo, slab,...  10.4 us
    pallas_call x2, Pallas kernels, run_filter(): pl.pallas_call(functools.partial(filter_kernel, first, halo, slab), in_sp...  9.23 us
    unnamed x24, local copies, waits for them, and re-layouts  9.02 us
  transfers between devices with their start and end apart: 2, of which 2 were waited for; matrix products, arithmetic and copies ran while one was open for 0% of the time, Pallas kernels for 2%

profile of v3, /device:TPU:8, one launch (start us, length us, event | category | flops | bytes accessed | tf_op | source)
XLA Modules:
  0.0 156.8 jit_solution(242994760521110927)
XLA Ops:
  0.0 0.0 copy-start
  0.0 1.2 copy-done
  1.2 1.3 shard_map.64
  2.5 0.0 copy-start.10
  2.5 0.0 copy-start.11
  2.5 6.4 %all-to-all-start = ((f32[16,1,64,256]{3,2,1,0:T(8,128)}), f32[16,1,64,256]{3,2,1,0:T(8,128)S(1)}, u32[]{:S(2)}, u32[]{:S(2)}) async-start(f32[16,1,64,256]{3,2,1,0:T(8,128)} %bitcast.2), calls=%async_computation | async-start | bytes 2097152 | tf_op jit(solution)/shard_map/all_to_all | solution.py:505
  9.0 0.0 copy-done.10
  9.0 0.0 copy-done.11
  9.0 0.0 copy-start.1
  9.0 0.1 fusion
  9.1 0.5 copy-done.1
  9.6 2.9 %shard_map.65 = (f32[1024,256]{1,0:T(8,128)S(1)}, f32[1024,256]{1,0:T(8,128)S(1)}, f32[1024,256]{1,0:T(8,128)S(1)}) custom-call(f32[16]{0:T(128)S(1)} %copy-done.1, bf16[256,640]{1,0:T(8,128)(2,1)S(1)} %pad.5.code_ref), custom_call_target="tpu_custom_call" | custom-call | flops 15728640 | bytes 3145728 | tf_op jit(solution)/shard_map/pallas_call | solution.py:98
  12.6 0.0 copy-start.2
  12.6 1.0 copy-done.2
  13.6 19.6 %all-to-all-done.refs_0_ = f32[16,1,64,256]{3,2,1,0:T(8,128)S(1)} async-done(((f32[16,1,64,256]{3,2,1,0:T(8,128)}), f32[16,1,64,256]{3,2,1,0:T(8,128)S(1)}, u32[]{:S(2)}, u32[]{:S(2)}) %all-to-all-start) | async-done | bytes 1048608 | tf_op jit(solution)/shard_map/all_to_all | solution.py:505
  33.2 0.0 copy-start.3
  33.2 1.2 copy-done.3
  34.4 1.9 %copy-done.4 = bf16[3,2,512,512]{3,2,1,0:T(8,128)(2,1)S(1)} copy-done((bf16[3,2,512,512]{3,2,1,0:T(8,128)(2,1)S(1)}, bf16[3,2,512,512]{3,2,1,0:T(8,128)(2,1)}, u32[]{:S(2)}) %copy-start.4) | copy-done | bytes 3145752
  36.3 0.9 copy-done.6
  37.3 5.2 %shard_map.66 = (f32[16,1,19,8,128]{4,3,2,1,0:T(8,128)}, f32[1,1024,256]{2,1,0:T(8,128)S(1)}) custom-call(f32[16,1,64,256]{3,2,1,0:T(8,128)S(1)} %all-to-all-done.refs_0_, bf16[2,256,256]{2,1,0:T(8,128)(2,1)S(1)} %copy-done.6, bf16[3,2,512,512]{3,2,1,0:T(8,128)(2,1)S(1)} %copy-done.4, f32[1024,256]{1,0:T(8,128)S(1)} %get-tuple-element.14.refs_3_, ...), custom_call_target="tpu_custom_call" | custom-call | flops 2415919104 | bytes 2097152 | tf_op jit(solution)/shard_map/pallas_call | solution.py:288
  42.5 0.0 copy-start.8
  42.5 1.0 copy-done.8
  43.4 5.7 %all-to-all-start.1 = ((f32[16,1,19,8,128]{4,3,2,1,0:T(8,128)}), f32[16,1,19,8,128]{4,3,2,1,0:T(8,128)S(1)}, u32[]{:S(2)}, u32[]{:S(2)}) async-start(f32[16,1,19,8,128]{4,3,2,1,0:T(8,128)} %get-tuple-element.16), calls=%async_computation.1 | async-start | bytes 2490368 | tf_op jit(solution)/shard_map/all_to_all | solution.py:505
  49.1 28.2 %all-to-all-done.1 = f32[16,1,19,8,128]{4,3,2,1,0:T(8,128)S(1)} async-done(((f32[16,1,19,8,128]{4,3,2,1,0:T(8,128)}), f32[16,1,19,8,128]{4,3,2,1,0:T(8,128)S(1)}, u32[]{:S(2)}, u32[]{:S(2)}) %all-to-all-start.1) | async-done | bytes 1245216 | tf_op jit(solution)/shard_map/all_to_all | solution.py:505
  77.4 4.7 %shard_map.67 = (f32[16,64,256]{2,1,0:T(8,128)S(1)}, f32[16,72,256]{2,1,0:T(8,128)S(1)}, f32[16,72,256]{2,1,0:T(8,128)S(1)}, f32[16,72,256]{2,1,0:T(8,128)S(1)}) custom-call(s32[1]{0:T(128)} %bitcast.start_ref, f32[16,19,8,128]{3,2,1,0:T(8,128)S(1)} %bitcast.9), custom_call_target="tpu_custom_call" | custom-call | flops 39321600 | bytes 10485760 | tf_op jit(solution)/shard_map/pallas_call | solution.py:482
  82.1 30.5 %all_to_all.20.refs_0_ = f32[16,1,64,256]{3,2,1,0:T(8,128)S(1)} all-to-all(f32[16,1,64,256]{3,2,1,0:T(8,128)S(1)} %bitcast.12), channel_id=1, replica_groups=mesh['groups'=2,'gy'=16] {'gy'}, dimensions={0} | all-to-all | bytes 2097152 | tf_op jit(solution)/shard_map/all_to_all | solution.py:505
  112.6 0.0 copy-done.7
  112.6 0.0 copy-done.5
  112.6 1.2 copy-done.9
  113.8 4.0 %shard_map.68 = f32[16,1,18,8,128]{4,3,2,1,0:T(8,128)S(1)} custom-call(f32[16,1,64,256]{3,2,1,0:T(8,128)S(1)} %all_to_all.20.refs_0_, bf16[2,256,256]{2,1,0:T(8,128)(2,1)S(1)} %copy-done.7, bf16[3,2,512,512]{3,2,1,0:T(8,128)(2,1)S(1)} %copy-done.5, f32[1,1024,256]{2,1,0:T(8,128)S(1)} %copy-done.9, f32[1024,256]{1,0:T(8,128)S(1)} %get-tuple-element.19.refs_4_), custom_call_target="tpu_custom_call" | custom-call | flops 2415919104 | bytes 2097152 | tf_op jit(solution)/shard_map/pallas_call | solution.py:288
  117.9 33.2 %all_to_all.21 = f32[16,1,18,8,128]{4,3,2,1,0:T(8,128)S(1)} all-to-all(f32[16,1,18,8,128]{4,3,2,1,0:T(8,128)S(1)} %shard_map.68), channel_id=1, replica_groups=mesh['groups'=2,'gy'=16] {'gy'}, dimensions={0} | all-to-all | bytes 2359296 | tf_op jit(solution)/shard_map/all_to_all | solution.py:505
  151.0 5.7 %shard_map.69 = f32[1024,256]{1,0:T(8,128)} custom-call(s32[1]{0:T(128)} %bitcast.start_ref, f32[16,18,8,128]{3,2,1,0:T(8,128)S(1)} %bitcast.10, f32[16,72,256]{2,1,0:T(8,128)S(1)} %get-tuple-element.20.refs_0_, f32[16,72,256]{2,1,0:T(8,128)S(1)} %get-tuple-element.21.refs_1_, f32[16,72,256]{2,1,0:T(8,128)S(1)} %get-tuple-element.22.refs_2_), custom_call_target="tpu_custom_call" | custom-call | flops 35389440 | bytes 9437184 | tf_op jit(solution)/shard_map/pallas_call | solution.py:482
  (6 shorter events, 0.0 us)
Async XLA Ops:
  0.0 1.2 copy-start
  2.5 6.5 %copy-start.10 = (s32[513,129]{0,1:T(8,128)S(1)}, s32[513,129]{0,1:T(8,128)}, u32[]{:S(2)}) copy-start(s32[513,129]{0,1:T(8,128)} %param.8) | copy-start | bytes 794128
  2.5 6.5 %copy-start.11 = (s32[513,129]{0,1:T(8,128)S(1)}, s32[513,129]{0,1:T(8,128)}, u32[]{:S(2)}) copy-start(s32[513,129]{0,1:T(8,128)} %param.9) | copy-start | bytes 794128
  2.5 30.7 %all-to-all-start = ((f32[16,1,64,256]{3,2,1,0:T(8,128)}), f32[16,1,64,256]{3,2,1,0:T(8,128)S(1)}, u32[]{:S(2)}, u32[]{:S(2)}) async-start(f32[16,1,64,256]{3,2,1,0:T(8,128)} %bitcast.2), calls=%async_computation | async-start | bytes 2097152 | tf_op jit(solution)/shard_map/all_to_all | solution.py:505
  9.0 0.7 copy-start.1
  12.6 1.0 copy-start.2
  33.2 1.2 copy-start.3
  34.4 1.9 %copy-start.4 = (bf16[3,2,512,512]{3,2,1,0:T(8,128)(2,1)S(1)}, bf16[3,2,512,512]{3,2,1,0:T(8,128)(2,1)}, u32[]{:S(2)}) copy-start(bf16[3,2,512,512]{3,2,1,0:T(8,128)(2,1)} %constant.18.clone.refs_2_) | copy-start | bytes 9437188
  36.3 0.9 copy-start.6
  42.5 1.0 copy-start.8
  43.4 69.2 %copy-start.7 = (bf16[2,256,256]{2,1,0:T(8,128)(2,1)S(1)}, bf16[2,256,256]{2,1,0:T(8,128)(2,1)}, u32[]{:S(2)}) copy-start(bf16[2,256,256]{2,1,0:T(8,128)(2,1)} %constant.17.clone.refs_1_) | copy-start | bytes 786436
  43.4 34.0 %all-to-all-start.1 = ((f32[16,1,19,8,128]{4,3,2,1,0:T(8,128)}), f32[16,1,19,8,128]{4,3,2,1,0:T(8,128)S(1)}, u32[]{:S(2)}, u32[]{:S(2)}) async-start(f32[16,1,19,8,128]{4,3,2,1,0:T(8,128)} %get-tuple-element.16), calls=%async_computation.1 | async-start | bytes 2490368 | tf_op jit(solution)/shard_map/all_to_all | solution.py:505
  77.4 35.2 %copy-start.5 = (bf16[3,2,512,512]{3,2,1,0:T(8,128)(2,1)S(1)}, bf16[3,2,512,512]{3,2,1,0:T(8,128)(2,1)}, u32[]{:S(2)}) copy-start(bf16[3,2,512,512]{3,2,1,0:T(8,128)(2,1)} %constant.18.clone.refs_2_) | copy-start | bytes 9437188
  112.6 1.2 copy-start.9
